TPU v7x, 256 devices: a whole 4x4x8 slice. The times are simulated.
256 devices in a mesh: rep: 64 (over z, y, core), mdl: 4 (over x).
Axes of the slice: x: 4, y: 4, z: 8, core: 2. Of those that a mesh axis runs over, the one named last changes fastest.
Arguments:
- grads: bfloat16 [64, 512, 128, 128], P('rep', 'mdl'), may hold values from -3600 to 3600
- momentum: bfloat16 [64, 512, 128, 128], P('rep', 'mdl'), may hold values from -6 to 6
- weight: bfloat16 [512, 128, 128], P('mdl'), may hold values from -6 to 6
- select: int32 [512, 4], P('mdl'), may hold values from 0 to 63, all different within a row
Outputs:
- new_weight: bfloat16 [512, 128, 128], P('mdl')
- new_momentum: bfloat16 [64, 512, 128, 128], P('rep', 'mdl')
Inputs may be any that keep to these rules, and one draw needn't show every extreme that they name: `select`: each row names 4 different blocks.
All inputs are finite; a program needn't handle non-finite values.
Results may differ from a plain program's by a relative error of at most 0.001.
Values may be sent and summed in bfloat16 or wider, within the bound.
No kernel may reach another device: no remote copies, remote signals or barrier semaphores. Data moves between devices by JAX's collectives and lax.ppermute only.
A program may use at most 128 MiB of HBM per device.

v0:
```python
import jax
import jax.numpy as jnp
from jax import lax
from jax.sharding import PartitionSpec as P

GROUP = 128
FB = 16
NBS = 8
NBLK = 64


momentum_retention = 0.9
learn_rate = 0.1
eps = 1e-06


def dct_matrix(length):
    freq = jnp.arange(length, dtype=jnp.float32)[:, None]
    sample = jnp.arange(length, dtype=jnp.float32)[None, :]
    factor = jnp.where(freq == 0, jnp.sqrt(1.0 / length), jnp.sqrt(2.0 / length))
    return factor * jnp.cos(jnp.pi * (2.0 * sample + 1.0) * freq / (2.0 * length))


def to_blocks(groups):
    total = groups.shape[0]
    return (
        groups.reshape(total, NBS, FB, NBS, FB)
        .transpose(0, 1, 3, 2, 4)
        .reshape(total, NBLK, FB * FB)
    )


def from_blocks(block_tiles):
    total = block_tiles.shape[0]
    return (
        block_tiles.reshape(total, NBS, NBS, FB, FB)
        .transpose(0, 1, 3, 2, 4)
        .reshape(total, GROUP, GROUP)
    )


def forward_cosine(transform, groups):
    left = jnp.einsum("kn,cnm->ckm", transform, groups, precision=lax.Precision.HIGHEST)
    return jnp.einsum("ckm,lm->ckl", left, transform, precision=lax.Precision.HIGHEST)


def inverse(transform, spectrum):
    left = jnp.einsum("kn,ckl->cnl", transform, spectrum, precision=lax.Precision.HIGHEST)
    return jnp.einsum("cnl,lm->cnm", left, transform, precision=lax.Precision.HIGHEST)


def decode(transform, grand_totals, select, weight):
    indicator_matrix = (
        select[:, :, None] == jnp.arange(NBLK, dtype=jnp.int32)[None, None, :]
    ).astype(jnp.float32)
    complete_spectrum = jnp.einsum(
        "dwk,dwh->dkh", indicator_matrix, grand_totals, precision=lax.Precision.HIGHEST
    )
    decoded = inverse(transform, from_blocks(complete_spectrum))
    inv_rms = lax.rsqrt(jnp.mean(decoded * decoded, axis=(1, 2), keepdims=True) + eps)
    return (weight.astype(jnp.float32) - learn_rate * decoded * inv_rms).astype(jnp.bfloat16)


def per_device(grads, momentum, weight, select):
    transform = dct_matrix(GROUP)
    shard_groups = grads.shape[1]
    entry_count = float(shard_groups * lax.axis_size("mdl") * GROUP * GROUP)
    grad_wide = grads[0].astype(jnp.float32)
    square_sum = lax.psum(jnp.sum(grad_wide * grad_wide), "mdl")
    clip = jnp.minimum(1.0, lax.rsqrt(square_sum / entry_count))
    moment = momentum_retention * momentum[0].astype(jnp.float32) + clip * grad_wide
    block_tiles = to_blocks(forward_cosine(transform, moment))
    coeffs = jnp.take_along_axis(block_tiles, select[:, :, None], axis=1)
    retain = 1.0 - jnp.any(
        select[:, :, None] == jnp.arange(NBLK, dtype=jnp.int32)[None, None, :], axis=1
    ).astype(jnp.float32)
    residual = from_blocks(block_tiles * retain[:, :, None])
    new_momentum = inverse(transform, residual).astype(jnp.bfloat16)[None]
    owned = shard_groups // lax.axis_size("rep")
    first_row = lax.axis_index("rep") * owned
    owned_sums = lax.psum_scatter(coeffs, "rep", scatter_dimension=0, tiled=True)
    owned_select = lax.dynamic_slice_in_dim(select, first_row, owned, 0)
    owned_weight = lax.dynamic_slice_in_dim(weight, first_row, owned, 0)
    updated = decode(transform, owned_sums, owned_select, owned_weight)
    new_weight = lax.all_gather(updated, "rep", axis=0, tiled=True)
    return (new_weight, new_momentum)


def solution(mesh):
    return jax.shard_map(
        per_device,
        mesh=mesh,
        in_specs=(
            P("rep", "mdl", None, None),
            P("rep", "mdl", None, None),
            P("mdl", None, None),
            P("mdl", None),
        ),
        out_specs=(P("mdl", None, None), P("rep", "mdl", None, None)),
        check_vma=False,
    )
```

profile of v0, /device:TPU:1, one launch (start us, length us, event | category | flops | bytes accessed | tf_op | source)
XLA Modules:
  0.0 370.0 jit_solution(8610459251448036813)
XLA Ops:
  7.2 0.7 compare_and_fusion
  7.9 0.7 bitcast_or_fusion
  8.6 4.9 %fusion = f32[]{:T(128)} fusion(bf16[1,128,128,128]{3,2,1,0:T(8,128)(2,1)} %param.4), kind=kLoop, calls=%fused_computation.3 | loop fusion | flops 6291455 | bytes 4194308 | tf_op jit(solution)/shard_map/reduce_sum | solution.py:69
  13.5 9.9 %psum.7 = f32[]{:T(128)} all-reduce(f32[]{:T(128)} %fusion), channel_id=1, replica_groups=mesh['rep'=64,'mdl'=4] {'mdl'}, use_global_device_ids=true, to_apply=%region_1.2 | all-reduce | flops 1 | bytes 8 | tf_op jit(solution)/shard_map/psum | solution.py:69
  24.5 17.6 %fusion.3 = f32[128,128,128]{2,1,0:T(8,128)S(1)} fusion(bf16[1,128,128,128]{3,2,1,0:T(8,128)(2,1)} %param.4, bf16[1,128,128,128]{3,2,1,0:T(8,128)(2,1)} %param.5, f32[]{:T(128)S(6)} %min.3, f32[128]{0:T(128)S(1)} %get-tuple-element.5, f32[128]{0:T(128)S(1)} %get-tuple-element.4), kind=kOutput, calls=%fused_computation.6 | convolution fusion | flops 3231760384 | bytes 16778244 | tf_op jit(solution)/shard_map/kn,cnm->ckm/dot_general | solution.py:43
  42.1 16.5 %fusion.7 = f32[128,128,128]{2,1,0:T(8,128)} fusion(f32[128,128,128]{2,1,0:T(8,128)S(1)} %fusion.3, f32[128]{0:T(128)S(1)} %get-tuple-element.5, f32[128]{0:T(128)S(1)} %get-tuple-element.4), kind=kOutput, calls=%fused_computation.9 | convolution fusion | flops 3221274624 | bytes 16778240 | tf_op jit(solution)/shard_map/ckm,lm->ckl/dot_general | solution.py:44
  58.6 9.3 %copy.38 = f32[128,128,128]{0,2,1:T(8,128)} copy(f32[128,128,128]{2,1,0:T(8,128)} %fusion.7) | data formatting | bytes 16777216 | tf_op jit(solution)/shard_map/ckm,lm->ckl/dot_general | solution.py:44
  67.9 7.8 %copy.39 = f32[128,8,8,16,16]{0,4,3,2,1:T(8,128)} copy(f32[128,8,8,16,16]{0,4,2,3,1:T(8,128)} %bitcast.51) | data formatting | bytes 16777216 | tf_op jit(solution)/shard_map/transpose | solution.py:28
  75.8 9.2 %copy.41 = f32[128,64,256]{2,1,0:T(8,128)} copy(f32[128,64,256]{0,2,1:T(8,128)} %bitcast.49) | data formatting | bytes 16777216 | tf_op jit(solution)/shard_map/reshape | solution.py:29
  85.0 6.1 %gather_fusion = f32[512,256]{1,0:T(8,128)S(1)} fusion(f32[128,64,256]{2,1,0:T(8,128)} %copy.41, s32[512]{0:T(512)S(1)} %reshape.75), kind=kCustom, calls=%fused_computation | custom fusion | bytes 1052672 | tf_op jit(solution)/shard_map/jit(take_along_axis)/gather | solution.py:73
  91.3 1.0 broadcast_select_fusion
  92.8 0.6 dynamic-slice
  94.0 180.6 %all-reduce.3.cloned.1.call-done = f32[128,4,256]{2,1,0:T(4,128)} async-done(((f32[128,4,256]{2,1,0:T(4,128)}), f32[128,4,256]{2,1,0:T(4,128)}) %all-reduce.3.cloned.1.call-update) | async-done | bytes 524304
  274.6 1.0 fusion.43
  276.0 0.3 copy.55
  276.7 0.6 convolution_bitcast_fusion
  277.2 0.7 multiply_reduce_fusion
  277.9 1.6 subtract_convert_fusion
  279.5 4.2 %mul.184 = f32[128,8,16,8,16]{0,4,3,2,1:T(8,128)} broadcast(f32[128,8,8]{0,2,1:T(8,128)S(1)} %subtract_bitcast_fusion), dimensions={0,1,3} | broadcast | bytes 8421376 | tf_op jit(solution)/shard_map/mul | solution.py:77
  283.7 9.3 %copy.45 = f32[128,128,128]{2,1,0:T(8,128)} copy(f32[128,128,128]{0,2,1:T(8,128)} %bitcast.50) | data formatting | bytes 16777216 | tf_op jit(solution)/shard_map/mul | solution.py:77
  293.0 17.3 %fusion.9 = f32[128,128,128]{2,1,0:T(8,128)S(1)} fusion(f32[128,128,128]{2,1,0:T(8,128)} %fusion.7, f32[128,128,128]{2,1,0:T(8,128)} %copy.45, f32[128]{0:T(128)S(1)} %get-tuple-element.5, f32[128]{0:T(128)S(1)} %get-tuple-element.4), kind=kOutput, calls=%fused_computation.11 | convolution fusion | flops 3223371776 | bytes 25166848 | tf_op jit(solution)/shard_map/kn,ckl->cnl/dot_general | solution.py:48
  310.3 15.7 %convert_bitcast_fusion = bf16[1,128,128,128]{3,2,1,0:T(8,128)(2,1)} fusion(f32[128,128,128]{2,1,0:T(8,128)S(1)} %fusion.9, f32[128]{0:T(128)S(1)} %get-tuple-element.5, f32[128]{0:T(128)S(1)} %get-tuple-element.4), kind=kOutput, calls=%fused_computation.15 | convolution fusion | flops 3223371776 | bytes 12583936 | tf_op jit(solution)/shard_map/cnl,lm->cnm/dot_general | solution.py:49
  326.0 32.4 %all-gather.2.cloned.1.call-done = bf16[128,128,128]{2,1,0:T(8,128)(2,1)} async-done(((bf16[2,128,128]{2,1,0:T(8,128)(2,1)}), bf16[128,128,128]{2,1,0:T(8,128)(2,1)}) %all-gather.2.cloned.1.call-update) | async-done | bytes 4194320 | tf_op jit(solution)/shard_map/all_gather | solution.py:85
  358.4 4.8 %copy.58 = bf16[128,128,128]{2,1,0:T(8,128)(2,1)} copy(bf16[128,128,128]{2,1,0:T(8,128)(2,1)} %all-gather.2.cloned.1.call-done) | data formatting | bytes 8388608
  (20 shorter events, 1.7 us)
Async XLA Ops:
  7.2 267.5 %all-reduce.3.cloned.1.call-start = ((), (), s32[]{:S(2)}) async-start(), calls=%async_computation.1 | async-start | bytes 1048576
  75.8 16.8 %copy-start = (s32[128,4]{0,1:T(4,128)S(1)}, s32[128,4]{0,1:T(4,128)}, u32[]{:S(2)}) copy-start(s32[128,4]{0,1:T(4,128)} %param.7) | copy-start | bytes 6148
  75.8 17.0 %copy-start.1 = (u32[256]{0:T(256)S(1)}, u32[256]{0:T(256)}, u32[]{:S(2)}) copy-start(u32[256]{0:T(256)} %constant.74) | copy-start | bytes 3076
  92.3 266.1 %all-gather.2.cloned.1.call-start = ((), (), s32[]{:S(2)}) async-start(), calls=%async_computation | async-start | bytes 4259840 | tf_op jit(solution)/shard_map/all_gather | solution.py:85
Sparse Core Ops, SparseCore 0:
  92.4 182.1 all-reduce.2
  279.6 78.7 all-gather.1
where the time goes:
time: 371 us; the launch traced here: 370 us
  waiting for transfers between devices  213 us (57%)
  matrix products  69.3 us (19%)
  local copies, waits for them, and re-layouts  53 us (14%)
  between operations  15.5 us (4%)
  blocking collectives  9.91 us (3%)
  other arithmetic  8.94 us (2%)
    unnamed x3, waiting for transfers between devices  181 us
    all_gather x1, waiting for transfers between devices, per_device(): new_weight = lax.all_gather(updated, 'rep', axis=0, tiled=True)  32.4 us
    dot_general x2, matrix products, inverse(): jnp.einsum('kn,ckl->cnl', transform, spectrum, precision=lax.Precision.HI...  17.9 us
    dot_general x1, matrix products, forward_cosine(): jnp.einsum('kn,cnm->ckm', transform, groups, precision=lax.Precision.HIGH...  17.6 us
    dot_general x1, matrix products, forward_cosine(): jnp.einsum('ckm,lm->ckl', left, transform, precision=lax.Precision.HIGHEST)  16.5 us
    dot_general x2, matrix products, inverse(): jnp.einsum('cnl,lm->cnm', left, transform, precision=lax.Precision.HIGHEST)  16.3 us
    mul x2, local copies, waits for them, and re-layouts, per_device(): residual = from_blocks(block_tiles * retain[:, :, None])  13.5 us
    psum x1, blocking collectives, per_device(): square_sum = lax.psum(jnp.sum(grad_wide * grad_wide), 'mdl')  9.91 us
  transfers between devices with their start and end apart: 2, of which 2 were waited for; matrix products, arithmetic and copies ran while one was open for 13% of the time, Pallas kernels for 0%

commit v1 on v0

v1 whole, which is shorter than its diff:
```python
import functools

import jax
import jax.numpy as jnp
import ml_dtypes
import numpy as np
from jax import lax
from jax.experimental import pallas as pl
from jax.experimental.pallas import tpu as pltpu
from jax.sharding import PartitionSpec as P

GROUP = 128
FB = 16
NBS = 8
KSEL = 4
REPS = 64
CHIPS = 32
PAIRS = 64
HALF = 32
momentum_retention = 0.9
learn_rate = 0.1
eps = 1e-06


def dct_tables():
    freq = np.arange(GROUP, dtype=np.float64)[:, None]
    sample = np.arange(GROUP, dtype=np.float64)[None, :]
    factor = np.where(freq == 0, np.sqrt(1.0 / GROUP), np.sqrt(2.0 / GROUP))
    full = factor * np.cos(np.pi * (2.0 * sample + 1.0) * freq / (2.0 * GROUP))
    high = full.astype(ml_dtypes.bfloat16)
    low = (full - high.astype(np.float64)).astype(ml_dtypes.bfloat16)
    return high, low


def split(wide):
    high = wide.astype(jnp.bfloat16)
    low = (wide - high.astype(jnp.float32)).astype(jnp.bfloat16)
    return high, low


def dot(a, b, dims=(((1,), (0,)), ((), ()))):
    return lax.dot_general(a, b, dims, preferred_element_type=jnp.float32)


NT = (((1,), (1,)), ((), ()))
TN = (((0,), (0,)), ((), ()))


def gather_rows(table, blocks):
    return jnp.concatenate(
        [table[pl.ds(pl.multiple_of(b * FB, FB), FB), :] for b in blocks], axis=0
    )


def blocks_of(sel, pair):
    picked = [sel[pair * 8 + q] for q in range(8)]
    return [b // NBS for b in picked], [b % NBS for b in picked]


def square_kernel(g, out):
    @pl.when(pl.program_id(0) == 0)
    def _():
        out[...] = jnp.zeros_like(out)

    wide = g[...].astype(jnp.float32)
    wide = (wide * wide).reshape(-1, 8, GROUP)
    out[...] += jnp.sum(wide, axis=0)


def square_sums(grads):
    step = 16
    groups = grads.shape[0]
    return pl.pallas_call(
        square_kernel,
        grid=(groups // step,),
        in_specs=[pl.BlockSpec((step, GROUP, GROUP), lambda i: (i, 0, 0))],
        out_specs=pl.BlockSpec((8, GROUP), lambda i: (0, 0)),
        out_shape=jax.ShapeDtypeStruct((8, GROUP), jnp.float32),
        cost_estimate=pl.CostEstimate(flops=4 << 20, bytes_accessed=4 << 20, transcendentals=0),
        name="square_sums",
    )(grads)


def forward_kernel(step, sel, off, g, m, t_high, t_low, cg, cm):
    lane = lax.broadcasted_iota(jnp.int32, (FB, GROUP), 1) // FB
    base = (off[0] + pl.program_id(0)) * step
    for p in range(step):
        rows, cols = blocks_of(sel, base + p)
        row_high, row_low = gather_rows(t_high, rows), gather_rows(t_low, rows)
        col_high, col_low = gather_rows(t_high, cols), gather_rows(t_low, cols)
        picked = []
        for s in range(2):
            both = jnp.concatenate([g[2 * p + s], m[2 * p + s]], axis=1)
            own = slice(64 * s, 64 * s + 64)
            left = jnp.concatenate([row_high[own], row_low[own]], axis=0)
            prod = dot(left, both)
            picked.append(prod[:64] + prod[64:])
        left = jnp.concatenate(picked, axis=0)
        left = jnp.concatenate([left[:, :GROUP], left[:, GROUP:]], axis=0)
        high, low = split(left)
        lhs = jnp.concatenate([high, low], axis=1)
        rhs = jnp.concatenate(
            [
                jnp.concatenate([col_high, col_high], axis=1),
                jnp.concatenate([col_low, jnp.zeros_like(col_low)], axis=1),
            ],
            axis=0,
        )
        prod = dot(lhs, rhs, NT)
        prod = prod[:, :GROUP] + prod[:, GROUP:]
        for at, ref in ((0, cg), (GROUP, cm)):
            tile = prod[at : at + FB]
            for q in range(1, 8):
                tile = jnp.where(lane == q, prod[at + FB * q : at + FB * q + FB], tile)
            ref[p] = tile


def forward(sel, half, grads, momentum, t_high, t_low):
    step = 4
    table = pl.BlockSpec((GROUP, GROUP), lambda i, sel, off: (0, 0))
    groups = pl.BlockSpec((2 * step, GROUP, GROUP), lambda i, sel, off: (off[0] + i, 0, 0))
    tiles = pl.BlockSpec((step, FB, GROUP), lambda i, sel, off: (i, 0, 0))
    shape = jax.ShapeDtypeStruct((HALF, FB, GROUP), jnp.float32)
    return pl.pallas_call(
        functools.partial(forward_kernel, step),
        grid_spec=pltpu.PrefetchScalarGridSpec(
            num_scalar_prefetch=2,
            grid=(HALF // step,),
            in_specs=[groups, groups, table, table],
            out_specs=[tiles, tiles],
        ),
        out_shape=[shape, shape],
        cost_estimate=pl.CostEstimate(flops=2 << 30, bytes_accessed=5 << 20, transcendentals=0),
        name="forward_cosine",
    )(sel, half * (HALF // step), grads, momentum, t_high, t_low)


def decode_pair(coeffs, rows, cols, t_high, t_low):
    lane = lax.broadcasted_iota(jnp.int32, (FB, GROUP), 1) // FB
    row_high, row_low = gather_rows(t_high, rows), gather_rows(t_low, rows)
    col_high, col_low = gather_rows(t_high, cols), gather_rows(t_low, cols)
    none = jnp.zeros((FB, GROUP), jnp.float32)
    parts = jnp.concatenate([jnp.where(lane == q, coeffs, none) for q in range(8)], axis=0)
    high, low = split(parts)
    lhs = jnp.concatenate([high, low], axis=1)
    rhs = jnp.concatenate(
        [
            jnp.concatenate([col_high, col_low], axis=1),
            jnp.concatenate([col_high, jnp.zeros_like(col_low)], axis=1),
        ],
        axis=0,
    )
    prod = dot(lhs, rhs)
    high, low = split(prod[:, :GROUP] + prod[:, GROUP:])
    result = []
    for s in range(2):
        own = slice(64 * s, 64 * s + 64)
        left = jnp.concatenate([row_high[own], row_high[own], row_low[own]], axis=0)
        right = jnp.concatenate([high[own], low[own], high[own]], axis=0)
        result.append(dot(left, right, TN))
    return result


def momentum_kernel(step, sel, off, clip, g, m, coeffs, t_high, t_low, _, out):
    base = (off[0] + pl.program_id(0)) * step
    for p in range(step):
        rows, cols = blocks_of(sel, base + p)
        for s, taken in enumerate(decode_pair(coeffs[p], rows, cols, t_high, t_low)):
            wide = momentum_retention * m[2 * p + s].astype(jnp.float32)
            wide += clip[0] * g[2 * p + s].astype(jnp.float32)
            out[2 * p + s] = (wide - taken).astype(jnp.bfloat16)


def weight_kernel(step, sel, off, w, coeffs, t_high, t_low, _, out):
    base = (off[0] + pl.program_id(0)) * step
    for p in range(step):
        rows, cols = blocks_of(sel, base + p)
        for s, taken in enumerate(decode_pair(coeffs[p], rows, cols, t_high, t_low)):
            wide = w[2 * p + s].astype(jnp.float32) - taken
            out[2 * p + s] = wide.astype(jnp.bfloat16)


def decode_half(kernel, scalars, half, arrays, coeffs, t_high, t_low, before, name):
    step = 4
    table = pl.BlockSpec((GROUP, GROUP), lambda i, sel, off, *_: (0, 0))
    groups = pl.BlockSpec((2 * step, GROUP, GROUP), lambda i, sel, off, *_: (off[0] + i, 0, 0))
    tiles = pl.BlockSpec((step, FB, GROUP), lambda i, *_: (i, 0, 0))
    scalars = (scalars[0], half * (HALF // step), *scalars[1:])
    operands = (*scalars, *arrays, coeffs, t_high, t_low)
    specs = [groups] * len(arrays) + [tiles, table, table]
    if before is None:
        inner = kernel
        kernel = lambda *refs: inner(*refs[:-1], None, refs[-1])
        aliases = {}
    else:
        aliases = {len(operands): 0}
        operands += (before,)
        specs.append(pl.BlockSpec(memory_space=pl.ANY))
    return pl.pallas_call(
        kernel,
        grid_spec=pltpu.PrefetchScalarGridSpec(
            num_scalar_prefetch=len(scalars),
            grid=(HALF // step,),
            in_specs=specs,
            out_specs=groups,
        ),
        out_shape=jax.ShapeDtypeStruct((2 * PAIRS, GROUP, GROUP), jnp.bfloat16),
        input_output_aliases=aliases,
        cost_estimate=pl.CostEstimate(flops=2 << 30, bytes_accessed=(2 << 20) * (1 + len(arrays)), transcendentals=0),
        name=name,
    )(*operands)


def total_kernel(parts, out):
    total = jnp.sum(parts[...], axis=0)
    lane = lax.broadcasted_iota(jnp.int32, (FB, GROUP), 1)
    square = total * total
    first = jnp.sum(jnp.where(lane < 64, square, 0.0))
    second = jnp.sum(jnp.where(lane < 64, 0.0, square))
    mean = jnp.where(lane < 64, first, second) / (GROUP * GROUP)
    out[...] = jnp.broadcast_to(learn_rate * total * lax.rsqrt(mean + eps), out.shape)


def scaled_totals(parts):
    return pl.pallas_call(
        total_kernel,
        out_shape=jax.ShapeDtypeStruct((CHIPS, FB, GROUP), jnp.float32),
        name="scaled_totals",
    )(parts)


def per_device(grads, momentum, weight, select):
    t_high, t_low = (jnp.asarray(table) for table in dct_tables())
    grads, momentum = grads[0], momentum[0]
    sel = select.reshape(-1)
    own = lax.rem(lax.axis_index("rep"), 2).astype(jnp.int32).reshape(1)
    other = 1 - own
    same_core = [list(range(c, REPS, 2)) for c in range(2)]
    swap_core = [(i, i ^ 1) for i in range(REPS)]
    swap = lambda x: lax.ppermute(x, "rep", swap_core)
    exchange = lambda x: lax.all_to_all(x, "rep", 0, 0, tiled=True, axis_index_groups=same_core)

    sums = square_sums(grads)
    square_sum = jnp.sum(sums).reshape(1, 1)
    square_sum += lax.ppermute(square_sum, "mdl", [(i, i ^ 1) for i in range(4)])
    square_sum += lax.ppermute(square_sum, "mdl", [(i, i ^ 2) for i in range(4)])
    entry_count = float(4 * grads.size)
    clip = jnp.minimum(1.0, lax.rsqrt(square_sum / entry_count))

    g_other, m_other = forward(sel, other, grads, momentum, t_high, t_low)
    g_own, m_own = forward(sel, own, grads, momentum, t_high, t_low)
    c_other = momentum_retention * m_other + clip[0, 0] * g_other
    c_own = momentum_retention * m_own + clip[0, 0] * g_own
    parts = exchange(c_own + swap(c_other))
    clip = clip.reshape(1)
    new_momentum = decode_half(
        functools.partial(momentum_kernel, 4), (sel, clip), other, (grads, momentum),
        c_other, t_high, t_low, None, "momentum_other",
    )
    mine = scaled_totals(parts)
    totals_own = exchange(mine)
    new_momentum = decode_half(
        functools.partial(momentum_kernel, 4), (sel, clip), own, (grads, momentum),
        c_own, t_high, t_low, new_momentum, "momentum_own",
    )
    totals_other = swap(totals_own)
    new_weight = decode_half(
        functools.partial(weight_kernel, 4), (sel,), own, (weight,),
        totals_own, t_high, t_low, None, "weight_own",
    )
    new_weight = decode_half(
        functools.partial(weight_kernel, 4), (sel,), other, (weight,),
        totals_other, t_high, t_low, new_weight, "weight_other",
    )
    return (new_weight, new_momentum[None])


def solution(mesh):
    return jax.shard_map(
        per_device,
        mesh=mesh,
        in_specs=(
            P("rep", "mdl", None, None),
            P("rep", "mdl", None, None),
            P("mdl", None, None),
            P("mdl", None),
        ),
        out_specs=(P("mdl", None, None), P("rep", "mdl", None, None)),
        check_vma=False,
    )
```

time: 371 us -> 114 us (0.31)
  waiting for transfers between devices: 213 us -> 0.89 us
  matrix products: 69.3 us -> 0 us
  Pallas kernels: 0 us -> 65.2 us
  local copies, waits for them, and re-layouts: 53 us -> 1.5 us
  starting transfers between devices: 0.3 us -> 15.6 us
  blocking collectives: 9.91 us -> 22.8 us
  between operations: 15.5 us -> 2.62 us
  other arithmetic: 8.94 us -> 4.17 us
    unnamed x3 -> x0, waiting for transfers between devices: 181 us -> none
    dot_general x7 -> x0, matrix products: 69.3 us -> none  [the longest x2 17.9 us: inverse(): jnp.einsum('kn,ckl->cnl', transform, spectrum, precision=lax.Precision.HI...]
    pallas_call x0 -> x8, Pallas kernels: none -> 65.2 us  [the longest x4 40.2 us: decode_half(): pl.pallas_call(kernel, grid_spec=pltpu.PrefetchScalarGridSpec(num_scalar_...]
    all_gather x1 -> x0, waiting for transfers between devices: 32.4 us -> none  [per_device(): new_weight = lax.all_gather(updated, 'rep', axis=0, tiled=True)]
    all_to_all x0 -> x1, blocking collectives: none -> 22.8 us  [per_device(): lax.all_to_all(x, 'rep', 0, 0, tiled=True, axis_index_groups=same_core)]
    mul x2 -> x0, local copies, waits for them, and re-layouts: 13.5 us -> none  [per_device(): residual = from_blocks(block_tiles * retain[:, :, None])]
    ppermute x0 -> x4, starting transfers between devices: none -> 11.4 us  [the longest x2 6.08 us: per_device(): swap = lambda x: lax.ppermute(x, 'rep', swap_core)]
    psum x1 -> x0, blocking collectives: 9.91 us -> none  [per_device(): square_sum = lax.psum(jnp.sum(grad_wide * grad_wide), 'mdl')]
  transfers between devices with their start and end apart: 2 -> 5, of which waited for: 2 -> 2; matrix products, arithmetic and copies ran while one was open for 13% -> 1% of each run, Pallas kernels for 0% -> 42%
where the time goes in v1:
time: 114 us; the launch traced here: 113 us
  Pallas kernels  65.2 us (57%)
  blocking collectives  22.8 us (20%)
  starting transfers between devices  15.6 us (14%)
  other arithmetic  4.17 us (4%)
  between operations  2.62 us (2%)
  local copies, waits for them, and re-layouts  1.5 us (1%)
    pallas_call x4, Pallas kernels, decode_half(): pl.pallas_call(kernel, grid_spec=pltpu.PrefetchScalarGridSpec(num_scalar_...  40.2 us
    all_to_all x1, blocking collectives, per_device(): lax.all_to_all(x, 'rep', 0, 0, tiled=True, axis_index_groups=same_core)  22.8 us
    pallas_call x2, Pallas kernels, forward(): pl.pallas_call(functools.partial(forward_kernel, step), grid_spec=pltpu.P...  16.9 us
    pallas_call x1, Pallas kernels, square_sums(): pl.pallas_call(square_kernel, grid=(groups // step,), in_specs=[pl.BlockS...  6.25 us
    ppermute x2, starting transfers between devices, per_device(): swap = lambda x: lax.ppermute(x, 'rep', swap_core)  6.08 us
    all_to_all x1, starting transfers between devices, per_device(): lax.all_to_all(x, 'rep', 0, 0, tiled=True, axis_index_groups=same_core)  4.2 us
    ppermute x1, starting transfers between devices, per_device(): lax.ppermute(square_sum, 'mdl', [(i, i ^ 2) for i in range(4)])  3.25 us
  transfers between devices with their start and end apart: 5, of which 2 were waited for; matrix products, arithmetic and copies ran while one was open for 1% of the time, Pallas kernels for 42%

profile of v1, /device:TPU:1, one launch (start us, length us, event | category | flops | bytes accessed | tf_op | source)
XLA Modules:
  0.0 112.8 jit_solution(5013920307579166665)
XLA Ops:
  0.6 6.3 %square_sums.1 = f32[8,128]{1,0:T(8,128)} custom-call(bf16[128,128,128]{2,1,0:T(8,128)(2,1)} %bitcast.8), custom_call_target="tpu_custom_call" | custom-call | flops 4194304 | bytes 4194304 | tf_op jit(solution)/shard_map/square_sums/pallas_call | solution.py:73
  6.9 1.3 %reduce_sum.9 = f32[]{:T(128)} reduce(f32[8,128]{1,0:T(8,128)} %square_sums.1, f32[]{:T(128)} %constant.27.clone.1), dimensions={0,1}, to_apply=%region_0.0 | reduce | flops 1023 | bytes 4104 | tf_op jit(solution)/shard_map/reduce_sum | solution.py:244
  8.2 2.0 %collective-permute-start = (f32[1,1]{1,0:T(1,128)}, f32[1,1]{1,0:T(1,128)}, u32[]{:S(2)}, u32[]{:S(2)}) collective-permute-start(f32[1,1]{1,0:T(1,128)} %bitcast.4), channel_id=1, source_target_pairs={{0,1},{1,0},{2,3},{3,2},{4,5},{5,4},{6,7},{7,6},{8,9},{9,8},{10,11... | collective-permute-start | bytes 20 | tf_op jit(solution)/shard_map/ppermute | solution.py:245
  10.3 0.1 copy.10
  10.4 0.7 reshape.20.sel.refs_0_
  11.0 8.5 %forward_cosine.3 = (f32[32,16,128]{2,1,0:T(8,128)}, f32[32,16,128]{2,1,0:T(8,128)}) custom-call(s32[512]{0:T(512)} %reshape.20.sel.refs_0_, s32[1]{0:T(128)} %bitcast.off.refs_1_, bf16[128,128,128]{2,1,0:T(8,128)(2,1)} %bitcast.9, bf16[128,128,128]{2,1,0:T(8,128)(2,1)} %bitcast.13, bf16[128,128]{1,0:T(8,128)(2,1)} %constant.30.clone.t_high.refs_4_.refs_6_, ...), custom_call_target="tpu_custom_call" | custom-call | flops 2147483648 | bytes 5242880 | tf_op jit(solution)/shard_map/forward_cosine/pallas_call | solution.py:124
  19.5 0.0 collective-permute-done
  20.8 3.3 %collective-permute-start.1 = (f32[1,1]{1,0:T(1,128)}, f32[1,1]{1,0:T(1,128)}, u32[]{:S(2)}, u32[]{:S(2)}) collective-permute-start(f32[1,1]{1,0:T(1,128)} %add.15), channel_id=1, source_target_pairs={{0,2},{1,3},{2,0},{3,1},{4,6},{5,7},{6,4},{7,5},{8,10},{9,11},{10,... | collective-permute-start | bytes 20 | tf_op jit(solution)/shard_map/ppermute | solution.py:246
  24.0 0.7 collective-permute-done.1
  25.4 1.1 multiply_add_fusion.refs_5_
  26.5 2.6 %collective-permute-start.2 = (f32[32,16,128]{2,1,0:T(8,128)S(1)}, f32[32,16,128]{2,1,0:T(8,128)S(1)}, u32[]{:S(2)}, u32[]{:S(2)}) collective-permute-start(f32[32,16,128]{2,1,0:T(8,128)S(1)} %multiply_add_fusion.refs_5_), channel_id=1, source_target_pairs={{0,4},{4,0},{8,12},{12,8},{16,20},{20,16},{24,28},{28,24},{32,36},... | collective-permute-start | bytes 786440 | tf_op jit(solution)/shard_map/ppermute | solution.py:240
  29.0 8.5 %forward_cosine.2 = (f32[32,16,128]{2,1,0:T(8,128)}, f32[32,16,128]{2,1,0:T(8,128)}) custom-call(s32[512]{0:T(512)} %reshape.20.sel.refs_0_, s32[1]{0:T(128)} %bitcast.1.off.refs_1_, bf16[128,128,128]{2,1,0:T(8,128)(2,1)} %bitcast.10, bf16[128,128,128]{2,1,0:T(8,128)(2,1)} %bitcast.14, bf16[128,128]{1,0:T(8,128)(2,1)} %constant.30.clone.t_high.refs_4_.refs_6_, ...), custom_call_target="tpu_custom_call" | custom-call | flops 2147483648 | bytes 5242880 | tf_op jit(solution)/shard_map/forward_cosine/pallas_call | solution.py:124
  37.5 0.0 collective-permute-done.2
  37.5 1.8 %fusion = (f32[32,16,128]{2,1,0:T(8,128)S(1)}, f32[32,16,128]{2,1,0:T(8,128)}) fusion(f32[32,16,128]{2,1,0:T(8,128)S(1)} %collective-permute-done.2, f32[32,16,128]{2,1,0:T(8,128)} %get-tuple-element.7, f32[]{:T(128)} %bitcast.5, f32[32,16,128]{2,1,0:T(8,128)} %get-tuple-element.6), kind=kLoop, calls=%fused_computation.2 | loop fusion | flops 262144 | bytes 1310724 | tf_op jit(solution)/shard_map/add | solution.py:254
  39.3 22.8 %all_to_all.10.parts = f32[32,16,128]{2,1,0:T(8,128)} all-to-all(f32[32,16,128]{2,1,0:T(8,128)S(1)} %get-tuple-element.10), channel_id=1, replica_groups={{0,8,16,24,32,40,48,56,64,72,80,88,96,104,112,120,128,136,144,152,160,1..., dimensions={0} | all-to-all | bytes 524288 | tf_op jit(solution)/shard_map/all_to_all | solution.py:241
  62.2 1.8 %scaled_totals.1 = f32[32,16,128]{2,1,0:T(8,128)} custom-call(f32[32,16,128]{2,1,0:T(8,128)} %all_to_all.10.parts), custom_call_target="tpu_custom_call" | custom-call | tf_op jit(solution)/shard_map/scaled_totals/pallas_call | solution.py:225
  64.0 4.2 %all-to-all-start.1 = ((f32[32,16,128]{2,1,0:T(8,128)}), f32[32,16,128]{2,1,0:T(8,128)S(1)}, u32[]{:S(2)}, u32[]{:S(2)}) async-start(f32[32,16,128]{2,1,0:T(8,128)} %scaled_totals.1), calls=%async_computation.1 | async-start | bytes 524288 | tf_op jit(solution)/shard_map/all_to_all | solution.py:241
  68.2 10.2 %momentum_other.1._ = bf16[128,128,128]{2,1,0:T(8,128)(2,1)} custom-call(s32[512]{0:T(512)} %reshape.20.sel.refs_0_, s32[1]{0:T(128)} %bitcast.off.refs_1_, f32[1]{0:T(128)} %bitcast.6.refs_2_.clip, bf16[128,128,128]{2,1,0:T(8,128)(2,1)} %bitcast.11, bf16[128,128,128]{2,1,0:T(8,128)(2,1)} %bitcast.15, f32[32,16,128]{2,1,0:T(8,128)} %copy-done.1, ...), custom_call_target="tpu_custom_call" | custom-call | flops 2147483648 | bytes 6291456 | tf_op jit(solution)/shard_map/momentum_other/pallas_call | solution.py:199
  78.4 0.2 all-to-all-done.1.refs_3_
  78.6 3.5 %collective-permute-start.3 = (f32[32,16,128]{2,1,0:T(8,128)S(1)}, f32[32,16,128]{2,1,0:T(8,128)S(1)}, u32[]{:S(2)}, u32[]{:S(2)}) collective-permute-start(f32[32,16,128]{2,1,0:T(8,128)S(1)} %all-to-all-done.1.refs_3_), channel_id=1, source_target_pairs={{0,4},{4,0},{8,12},{12,8},{16,20},{20,16},{24,28},{28,24},{32,36},... | collective-permute-start | bytes 786440 | tf_op jit(solution)/shard_map/ppermute | solution.py:240
  82.1 10.3 %momentum_own.1 = bf16[128,128,128]{2,1,0:T(8,128)(2,1)} custom-call(s32[512]{0:T(512)} %reshape.20.sel.refs_0_, s32[1]{0:T(128)} %bitcast.1.off.refs_1_, f32[1]{0:T(128)} %bitcast.6.refs_2_.clip, bf16[128,128,128]{2,1,0:T(8,128)(2,1)} %bitcast.12, bf16[128,128,128]{2,1,0:T(8,128)(2,1)} %bitcast.16, ...), custom_call_target="tpu_custom_call", output_to_operand_aliasing={{}: (8, {})} | custom-call | flops 2147483648 | bytes 6291456 | tf_op jit(solution)/shard_map/momentum_own/pallas_call | solution.py:199
  92.4 9.8 %weight_own.1._ = bf16[128,128,128]{2,1,0:T(8,128)(2,1)} custom-call(s32[512]{0:T(512)} %reshape.20.sel.refs_0_, s32[1]{0:T(128)} %bitcast.1.off.refs_1_, bf16[128,128,128]{2,1,0:T(8,128)(2,1)} %w.1, f32[32,16,128]{2,1,0:T(8,128)} %copy-done, bf16[128,128]{1,0:T(8,128)(2,1)} %constant.30.clone.t_high.refs_4_.refs_6_, ...), custom_call_target="tpu_custom_call" | custom-call | flops 2147483648 | bytes 4194304 | tf_op jit(solution)/shard_map/weight_own/pallas_call | solution.py:199
  102.2 0.7 copy-done.2
  102.9 9.8 %weight_other.1 = bf16[128,128,128]{2,1,0:T(8,128)(2,1)} custom-call(s32[512]{0:T(512)} %reshape.20.sel.refs_0_, s32[1]{0:T(128)} %bitcast.off.refs_1_, bf16[128,128,128]{2,1,0:T(8,128)(2,1)} %w.1, f32[32,16,128]{2,1,0:T(8,128)} %copy-done.2, bf16[128,128]{1,0:T(8,128)(2,1)} %constant.30.clone.t_high.refs_4_.refs_6_, ...), custom_call_target="tpu_custom_call", output_to_operand_aliasing={{}: (6, {})} | custom-call | flops 2147483648 | bytes 4194304 | tf_op jit(solution)/shard_map/weight_other/pallas_call | solution.py:199
  (8 shorter events, 0.0 us)
Async XLA Ops:
  0.6 9.6 %copy-start.3 = (s32[128,4]{0,1:T(4,128)S(1)}, s32[128,4]{0,1:T(4,128)}, u32[]{:S(2)}) copy-start(s32[128,4]{0,1:T(4,128)} %param.9) | copy-start | bytes 6148
  8.2 11.3 %collective-permute-start = (f32[1,1]{1,0:T(1,128)}, f32[1,1]{1,0:T(1,128)}, u32[]{:S(2)}, u32[]{:S(2)}) collective-permute-start(f32[1,1]{1,0:T(1,128)} %bitcast.4), channel_id=1, source_target_pairs={{0,1},{1,0},{2,3},{3,2},{4,5},{5,4},{6,7},{7,6},{8,9},{9,8},{10,11... | collective-permute-start | bytes 20 | tf_op jit(solution)/shard_map/ppermute | solution.py:245
  20.8 3.9 %collective-permute-start.1 = (f32[1,1]{1,0:T(1,128)}, f32[1,1]{1,0:T(1,128)}, u32[]{:S(2)}, u32[]{:S(2)}) collective-permute-start(f32[1,1]{1,0:T(1,128)} %add.15), channel_id=1, source_target_pairs={{0,2},{1,3},{2,0},{3,1},{4,6},{5,7},{6,4},{7,5},{8,10},{9,11},{10,... | collective-permute-start | bytes 20 | tf_op jit(solution)/shard_map/ppermute | solution.py:246
  26.5 11.1 %copy-start.1 = (f32[32,16,128]{2,1,0:T(8,128)}, f32[32,16,128]{2,1,0:T(8,128)S(1)}, u32[]{:S(2)}) copy-start(f32[32,16,128]{2,1,0:T(8,128)S(1)} %multiply_add_fusion.refs_5_) | copy-start | bytes 786436
  26.5 11.1 %collective-permute-start.2 = (f32[32,16,128]{2,1,0:T(8,128)S(1)}, f32[32,16,128]{2,1,0:T(8,128)S(1)}, u32[]{:S(2)}, u32[]{:S(2)}) collective-permute-start(f32[32,16,128]{2,1,0:T(8,128)S(1)} %multiply_add_fusion.refs_5_), channel_id=1, source_target_pairs={{0,4},{4,0},{8,12},{12,8},{16,20},{20,16},{24,28},{28,24},{32,36},... | collective-permute-start | bytes 786440 | tf_op jit(solution)/shard_map/ppermute | solution.py:240
  64.0 14.6 %all-to-all-start.1 = ((f32[32,16,128]{2,1,0:T(8,128)}), f32[32,16,128]{2,1,0:T(8,128)S(1)}, u32[]{:S(2)}, u32[]{:S(2)}) async-start(f32[32,16,128]{2,1,0:T(8,128)} %scaled_totals.1), calls=%async_computation.1 | async-start | bytes 524288 | tf_op jit(solution)/shard_map/all_to_all | solution.py:241
  78.6 13.8 %copy-start = (f32[32,16,128]{2,1,0:T(8,128)}, f32[32,16,128]{2,1,0:T(8,128)S(1)}, u32[]{:S(2)}) copy-start(f32[32,16,128]{2,1,0:T(8,128)S(1)} %all-to-all-done.1.refs_3_) | copy-start | bytes 786436
  78.6 23.6 %collective-permute-start.3 = (f32[32,16,128]{2,1,0:T(8,128)S(1)}, f32[32,16,128]{2,1,0:T(8,128)S(1)}, u32[]{:S(2)}, u32[]{:S(2)}) collective-permute-start(f32[32,16,128]{2,1,0:T(8,128)S(1)} %all-to-all-done.1.refs_3_), channel_id=1, source_target_pairs={{0,4},{4,0},{8,12},{12,8},{16,20},{20,16},{24,28},{28,24},{32,36},... | collective-permute-start | bytes 786440 | tf_op jit(solution)/shard_map/ppermute | solution.py:240
  102.2 0.7 copy-start.2

commit v2 on v1

v2 whole, which is shorter than its diff:
```python
import functools

import jax
import jax.numpy as jnp
import ml_dtypes
import numpy as np
from jax import lax
from jax.experimental import pallas as pl
from jax.experimental.pallas import tpu as pltpu
from jax.sharding import PartitionSpec as P

GROUP = 128
FB = 16
NBS = 8
KSEL = 4
REPS = 64
CHIPS = 32
PAIRS = 64
HALF = 32
momentum_retention = 0.9
learn_rate = 0.1
eps = 1e-06


def dct_tables():
    freq = np.arange(GROUP, dtype=np.float64)[:, None]
    sample = np.arange(GROUP, dtype=np.float64)[None, :]
    factor = np.where(freq == 0, np.sqrt(1.0 / GROUP), np.sqrt(2.0 / GROUP))
    full = factor * np.cos(np.pi * (2.0 * sample + 1.0) * freq / (2.0 * GROUP))
    high = full.astype(ml_dtypes.bfloat16)
    low = (full - high.astype(np.float64)).astype(ml_dtypes.bfloat16)
    return high, low


def split(wide):
    high = wide.astype(jnp.bfloat16)
    low = (wide - high.astype(jnp.float32)).astype(jnp.bfloat16)
    return high, low


def dot(a, b, dims=(((1,), (0,)), ((), ()))):
    return lax.dot_general(a, b, dims, preferred_element_type=jnp.float32)


NT = (((1,), (1,)), ((), ()))
TN = (((0,), (0,)), ((), ()))


def gather_rows(table, blocks):
    return jnp.concatenate(
        [table[pl.ds(pl.multiple_of(b * FB, FB), FB), :] for b in blocks], axis=0
    )


def blocks_of(sel, pair):
    picked = [sel[pair * 8 + q] for q in range(8)]
    return [b // NBS for b in picked], [b % NBS for b in picked]


ANY = pl.BlockSpec(memory_space=pl.ANY)
VMEM = pl.BlockSpec(memory_space=pltpu.VMEM)
SMEM = pl.BlockSpec(memory_space=pltpu.SMEM)
STEP = 8
CHUNKS = HALF // STEP
CHUNK_GROUPS = 2 * STEP


def square_kernel(g, out, buf, sem):
    chunks = sem.shape[0]
    size = g.shape[0] // chunks

    def load(c):
        part = pl.ds(c * size, size)
        return pltpu.make_async_copy(g.at[part], buf.at[part], sem.at[c])

    for c in range(chunks):
        load(c).start()

    def body(c, total):
        load(c).wait()
        wide = buf[pl.ds(c * size, size)].astype(jnp.float32)
        return total + jnp.sum((wide * wide).reshape(-1, 64, GROUP), axis=0)

    total = lax.fori_loop(0, chunks, body, jnp.zeros((64, GROUP), jnp.float32))
    out[...] = jnp.sum(total.reshape(8, 8, GROUP), axis=0)


def square_sums(grads):
    return pl.pallas_call(
        square_kernel,
        in_specs=[ANY],
        out_specs=VMEM,
        out_shape=jax.ShapeDtypeStruct((8, GROUP), jnp.float32),
        scratch_shapes=[pltpu.VMEM(grads.shape, grads.dtype), pltpu.SemaphoreType.DMA((8,))],
        compiler_params=pltpu.CompilerParams(vmem_limit_bytes=51 << 20),
        cost_estimate=pl.CostEstimate(flops=4 << 20, bytes_accessed=4 << 20, transcendentals=0),
        name="square_sums",
    )(grads)


def load_half(arrays, bufs, sem, base):
    def load(a, c):
        return pltpu.make_async_copy(
            arrays[a].at[pl.ds(2 * base + c * CHUNK_GROUPS, CHUNK_GROUPS)],
            bufs[a].at[pl.ds(c * CHUNK_GROUPS, CHUNK_GROUPS)],
            sem.at[a, c],
        )

    for c in range(CHUNKS):
        for a in range(len(arrays)):
            load(a, c).start()

    def wait(c):
        for a in range(len(arrays)):
            load(a, c).wait()

    return wait


def forward_pair(g, m, rows, cols, t_high, t_low):
    lane = lax.broadcasted_iota(jnp.int32, (FB, GROUP), 1) // FB
    row_high, row_low = gather_rows(t_high, rows), gather_rows(t_low, rows)
    col_high, col_low = gather_rows(t_high, cols), gather_rows(t_low, cols)
    picked = []
    for s in range(2):
        own = slice(64 * s, 64 * s + 64)
        left = jnp.concatenate([row_high[own], row_low[own]], axis=0)
        prod = dot(left, jnp.concatenate([g[s], m[s]], axis=1))
        picked.append(prod[:64] + prod[64:])
    left = jnp.concatenate(picked, axis=0)
    left = jnp.concatenate([left[:, :GROUP], left[:, GROUP:]], axis=0)
    high, low = split(left)
    lhs = jnp.concatenate([high, low], axis=1)
    rhs = jnp.concatenate(
        [
            jnp.concatenate([col_high, col_high], axis=1),
            jnp.concatenate([col_low, jnp.zeros_like(col_low)], axis=1),
        ],
        axis=0,
    )
    prod = dot(lhs, rhs, NT)
    tiles = []
    for at in (0, GROUP):
        tile = None
        for q in range(8):
            part = prod[at + FB * q : at + FB * q + FB]
            part = part[:, :GROUP] + part[:, GROUP:]
            tile = part if q == 0 else jnp.where(lane == q, part, tile)
        tiles.append(tile)
    return tiles


def forward_kernel(sel, off, g, m, t_high, t_low, cg, cm, g_buf, m_buf, sem):
    base = off[0] * HALF
    wait = load_half((g, m), (g_buf, m_buf), sem, base)

    def body(c, _):
        wait(c)
        for u in range(STEP):
            p = c * STEP + u
            rows, cols = blocks_of(sel, base + p)
            pair = pl.ds(2 * p, 2)
            cg[p], cm[p] = forward_pair(g_buf[pair], m_buf[pair], rows, cols, t_high, t_low)
        return 0

    lax.fori_loop(0, CHUNKS, body, 0)


def forward(sel, half, grads, momentum, t_high, t_low):
    shape = jax.ShapeDtypeStruct((HALF, FB, GROUP), jnp.float32)
    buf = pltpu.VMEM((2 * HALF, GROUP, GROUP), jnp.bfloat16)
    return pl.pallas_call(
        forward_kernel,
        in_specs=[SMEM, SMEM, ANY, ANY, VMEM, VMEM],
        out_specs=[VMEM, VMEM],
        out_shape=[shape, shape],
        scratch_shapes=[buf, buf, pltpu.SemaphoreType.DMA((2, CHUNKS))],
        compiler_params=pltpu.CompilerParams(vmem_limit_bytes=51 << 20),
        cost_estimate=pl.CostEstimate(flops=2 << 30, bytes_accessed=5 << 20, transcendentals=0),
        name="forward_cosine",
    )(sel, half, grads, momentum, t_high, t_low)


def clip_of(first, second):
    square_sum = jnp.sum(first + second)
    entry_count = float(4 * 2 * PAIRS * GROUP * GROUP)
    return jnp.minimum(1.0, lax.rsqrt(jnp.full((1, GROUP), square_sum) / entry_count))


def combine_kernel(first, second, g_other, m_other, g_own, m_own, c_other, c_own, clip):
    clip[...] = clip_of(first[...], second[...])
    scale = clip[...].reshape(1, 1, GROUP)
    c_other[...] = momentum_retention * m_other[...] + scale * g_other[...]
    c_own[...] = momentum_retention * m_own[...] + scale * g_own[...]


def combine(first, second, *tiles):
    shape = jax.ShapeDtypeStruct((HALF, FB, GROUP), jnp.float32)
    return pl.pallas_call(
        combine_kernel,
        in_specs=[VMEM] * 6,
        out_specs=[VMEM] * 3,
        out_shape=[shape, shape, jax.ShapeDtypeStruct((1, GROUP), jnp.float32)],
        input_output_aliases={2: 0, 4: 1},
        compiler_params=pltpu.CompilerParams(vmem_limit_bytes=8 << 20),
        cost_estimate=pl.CostEstimate(flops=1 << 20, bytes_accessed=1 << 20, transcendentals=0),
        name="combine",
    )(first, second, *tiles)


def decode_pair(coeffs, rows, cols, t_high, t_low, t_left):
    lane = lax.broadcasted_iota(jnp.int32, (FB, GROUP), 1) // FB
    row_of = jnp.zeros((FB, GROUP), jnp.int32)
    for q in range(8):
        row_of = jnp.where(lane == q, rows[q], row_of)
    parts = jnp.concatenate([jnp.where(row_of == b, coeffs, 0.0) for b in range(NBS)], axis=0)
    high, low = split(parts)
    left = dot(t_left[...], jnp.concatenate([high, low, high], axis=0))
    high, low = split(left)
    none = jnp.zeros((64, GROUP), jnp.bfloat16)

    def both(table):
        chosen = gather_rows(table, cols)
        return jnp.concatenate(
            [
                jnp.concatenate([chosen[:64], none], axis=1),
                jnp.concatenate([none, chosen[64:]], axis=1),
            ],
            axis=0,
        )

    col_high, col_low = both(t_high), both(t_low)
    result = dot(
        jnp.concatenate([high, low, high], axis=1),
        jnp.concatenate([col_high, col_high, col_low], axis=0),
    )
    return result[:, :GROUP], result[:, GROUP:]


def decode_kernel(count, sel, off, *refs):
    arrays, refs = refs[:count], refs[count:]
    scale, coeffs, t_high, t_low, t_left = refs[:5]
    out = refs[-(count + 4)]
    bufs = refs[-(count + 3) : -3]
    out_buf, sem, out_sem = refs[-3:]
    base = off[0] * HALF
    wait = load_half(arrays, bufs, sem, base)

    def store(c):
        return pltpu.make_async_copy(
            out_buf.at[pl.ds(c * CHUNK_GROUPS, CHUNK_GROUPS)],
            out.at[pl.ds(2 * base + c * CHUNK_GROUPS, CHUNK_GROUPS)],
            out_sem.at[c],
        )

    def body(c, _):
        wait(c)
        for u in range(STEP):
            p = c * STEP + u
            rows, cols = blocks_of(sel, base + p)
            for s, taken in enumerate(decode_pair(coeffs[p], rows, cols, t_high, t_low, t_left)):
                wide = bufs[0][2 * p + s].astype(jnp.float32)
                if count == 2:
                    wide = momentum_retention * bufs[1][2 * p + s].astype(jnp.float32) + scale[...] * wide
                out_buf[2 * p + s] = (wide - taken).astype(jnp.bfloat16)
        store(c).start()
        return 0

    lax.fori_loop(0, CHUNKS, body, 0)
    for c in range(CHUNKS):
        store(c).wait()


def decode_half(sel, half, arrays, scale, coeffs, tables, before, name):
    operands = (sel, half, *arrays, scale, coeffs, *tables)
    specs = [SMEM, SMEM] + [ANY] * len(arrays) + [VMEM] * 5
    aliases = {}
    if before is not None:
        aliases = {len(operands): 0}
        operands += (before,)
        specs.append(ANY)
    buf = pltpu.VMEM((2 * HALF, GROUP, GROUP), jnp.bfloat16)
    return pl.pallas_call(
        functools.partial(decode_kernel, len(arrays)),
        in_specs=specs,
        out_specs=ANY,
        out_shape=jax.ShapeDtypeStruct((2 * PAIRS, GROUP, GROUP), jnp.bfloat16),
        scratch_shapes=[buf] * (len(arrays) + 1)
        + [pltpu.SemaphoreType.DMA((len(arrays), CHUNKS)), pltpu.SemaphoreType.DMA((CHUNKS,))],
        input_output_aliases=aliases,
        compiler_params=pltpu.CompilerParams(vmem_limit_bytes=51 << 20),
        cost_estimate=pl.CostEstimate(flops=2 << 30, bytes_accessed=(2 << 20) * (1 + len(arrays)), transcendentals=0),
        name=name,
    )(*operands)


def total_kernel(parts, out):
    total = jnp.sum(parts[...], axis=0)
    lane = lax.broadcasted_iota(jnp.int32, (FB, GROUP), 1)
    square = total * total
    first = jnp.sum(jnp.where(lane < 64, square, 0.0))
    second = jnp.sum(jnp.where(lane < 64, 0.0, square))
    mean = jnp.where(lane < 64, first, second) / (GROUP * GROUP)
    out[...] = jnp.broadcast_to(learn_rate * total * lax.rsqrt(mean + eps), out.shape)


def scaled_totals(parts):
    return pl.pallas_call(
        total_kernel,
        in_specs=[VMEM],
        out_specs=VMEM,
        out_shape=jax.ShapeDtypeStruct((CHIPS, FB, GROUP), jnp.float32),
        compiler_params=pltpu.CompilerParams(vmem_limit_bytes=8 << 20),
        cost_estimate=pl.CostEstimate(flops=1 << 20, bytes_accessed=1 << 19, transcendentals=0),
        name="scaled_totals",
    )(parts)


def per_device(grads, momentum, weight, select):
    high, low = dct_tables()
    left = np.concatenate([high.T, high.T, low.T], axis=1)
    t_high, t_low, t_left = tables = tuple(jnp.asarray(table) for table in (high, low, left))
    grads, momentum = grads[0], momentum[0]
    sel = select.reshape(-1)
    own = lax.rem(lax.axis_index("rep"), 2).astype(jnp.int32).reshape(1)
    other = 1 - own
    same_core = [list(range(c, REPS, 2)) for c in range(2)]
    swap_core = [(i, i ^ 1) for i in range(REPS)]
    swap = lambda x: lax.ppermute(x, "rep", swap_core)
    exchange = lambda x: lax.all_to_all(x, "rep", 0, 0, tiled=True, axis_index_groups=same_core)

    sums = square_sums(grads)
    sums += lax.ppermute(sums, "mdl", [(i, i ^ 1) for i in range(4)])
    g_other, m_other = forward(sel, other, grads, momentum, t_high, t_low)
    sums, g_other, m_other = lax.optimization_barrier((sums, g_other, m_other))
    far = lax.ppermute(sums, "mdl", [(i, i ^ 2) for i in range(4)])
    g_own, m_own = forward(sel, own, grads, momentum, t_high, t_low)
    c_other, c_own, clip = combine(sums, far, g_other, m_other, g_own, m_own)
    chip, c_other, c_own = lax.optimization_barrier((c_own + swap(c_other), c_other, c_own))
    parts = exchange(chip)
    new_momentum = decode_half(
        sel, other, (grads, momentum), clip, c_other, tables, None, "momentum_other"
    )
    parts, new_momentum = lax.optimization_barrier((parts, new_momentum))
    mine, c_own = lax.optimization_barrier((scaled_totals(parts), c_own))
    totals_own = exchange(mine)
    new_momentum = decode_half(
        sel, own, (grads, momentum), clip, c_own, tables, new_momentum, "momentum_own"
    )
    totals_own, new_momentum = lax.optimization_barrier((totals_own, new_momentum))
    totals_other = swap(totals_own)
    new_weight = decode_half(sel, own, (weight,), clip, totals_own, tables, None, "weight_own")
    new_weight = decode_half(
        sel, other, (weight,), clip, totals_other, tables, new_weight, "weight_other"
    )
    return (new_weight, new_momentum[None])


def solution(mesh):
    return jax.shard_map(
        per_device,
        mesh=mesh,
        in_specs=(
            P("rep", "mdl", None, None),
            P("rep", "mdl", None, None),
            P("mdl", None, None),
            P("mdl", None),
        ),
        out_specs=(P("mdl", None, None), P("rep", "mdl", None, None)),
        check_vma=False,
    )
```

time: 114 us -> 78.7 us (0.69)
  blocking collectives: 22.8 us -> 0 us
  Pallas kernels: 65.2 us -> 42.7 us
  starting transfers between devices: 15.6 us -> 25.1 us
  waiting for transfers between devices: 0.89 us -> 8.82 us
  other arithmetic: 4.17 us -> 0.74 us
  between operations: 2.62 us -> 0.8 us
  local copies, waits for them, and re-layouts: 1.5 us -> 0.24 us
    all_to_all x1 -> x0, blocking collectives: 22.8 us -> none  [per_device(): lax.all_to_all(x, 'rep', 0, 0, tiled=True, axis_index_groups=same_core)]
    pallas_call x8 -> x9, Pallas kernels: 65.2 us -> 42.7 us  [the longest x4 28.8 us: decode_half(): pl.pallas_call(functools.partial(decode_kernel, len(arrays)), in_specs=sp...]
    all_to_all x1 -> x2, starting transfers between devices: 4.2 us -> 16.2 us  [per_device(): lax.all_to_all(x, 'rep', 0, 0, tiled=True, axis_index_groups=same_core)]
    all_to_all x1 -> x2, waiting for transfers between devices: 0.2 us -> 7.65 us  [per_device(): lax.all_to_all(x, 'rep', 0, 0, tiled=True, axis_index_groups=same_core)]
    add x2, other arithmetic: 2.86 us -> 0.74 us  [the longest x1 0.74 us: per_device(): c_own + swap(c_other)]
    ppermute x2, starting transfers between devices: 6.08 us -> 4.27 us  [per_device(): swap = lambda x: lax.ppermute(x, 'rep', swap_core)]
    reduce_sum x1 -> x0, other arithmetic: 1.32 us -> none  [per_device(): square_sum = jnp.sum(sums).reshape(1, 1)]
    ppermute x2, waiting for transfers between devices: 0.01 us -> 1.16 us  [per_device(): swap = lambda x: lax.ppermute(x, 'rep', swap_core)]
  transfers between devices with their start and end apart: 5 -> 6, of which waited for: 2 -> 3; matrix products, arithmetic and copies ran while one was open for 1% -> 0% of each run, Pallas kernels for 42% -> 41%
where the time goes in v2:
time: 78.7 us; the launch traced here: 78.4 us
  Pallas kernels  42.7 us (54%)
  starting transfers between devices  25.1 us (32%)
  waiting for transfers between devices  8.82 us (11%)
  between operations  0.8 us (1%)
    pallas_call x4, Pallas kernels, decode_half(): pl.pallas_call(functools.partial(decode_kernel, len(arrays)), in_specs=sp...  28.8 us
    all_to_all x2, starting transfers between devices, per_device(): lax.all_to_all(x, 'rep', 0, 0, tiled=True, axis_index_groups=same_core)  16.2 us
    pallas_call x2, Pallas kernels, forward(): pl.pallas_call(forward_kernel, in_specs=[SMEM, SMEM, ANY, ANY, VMEM, VMEM...  10.6 us
    all_to_all x2, waiting for transfers between devices, per_device(): lax.all_to_all(x, 'rep', 0, 0, tiled=True, axis_index_groups=same_core)  7.65 us
    ppermute x2, starting transfers between devices, per_device(): swap = lambda x: lax.ppermute(x, 'rep', swap_core)  4.27 us
    ppermute x1, starting transfers between devices, per_device(): far = lax.ppermute(sums, 'mdl', [(i, i ^ 2) for i in range(4)])  2.53 us
    pallas_call x1, Pallas kernels, square_sums(): pl.pallas_call(square_kernel, in_specs=[ANY], out_specs=VMEM, out_shape=j...  2.27 us
    ppermute x1, starting transfers between devices, per_device(): sums += lax.ppermute(sums, 'mdl', [(i, i ^ 1) for i in range(4)])  2.13 us
  transfers between devices with their start and end apart: 6, of which 3 were waited for; matrix products, arithmetic and copies ran while one was open for 0% of the time, Pallas kernels for 41%

profile of v2, /device:TPU:1, one launch (start us, length us, event | category | flops | bytes accessed | tf_op | source)
XLA Modules:
  0.0 78.4 jit_solution(16341625196162373451)
XLA Ops:
  0.6 0.0 copy-start.1
  0.6 0.0 copy-start.2
  0.7 2.3 %square_sums.1 = f32[8,128]{1,0:T(8,128)S(1)} custom-call(bf16[128,128,128]{2,1,0:T(8,128)(2,1)} %bitcast.4), custom_call_target="tpu_custom_call" | custom-call | flops 4194304 | bytes 4194304 | tf_op jit(solution)/shard_map/square_sums/pallas_call | solution.py:89
  2.9 2.1 %collective-permute-start = (f32[8,128]{1,0:T(8,128)S(1)}, f32[8,128]{1,0:T(8,128)S(1)}, u32[]{:S(2)}, u32[]{:S(2)}) collective-permute-start(f32[8,128]{1,0:T(8,128)S(1)} %square_sums.1), channel_id=1, source_target_pairs={{0,1},{1,0},{2,3},{3,2},{4,5},{5,4},{6,7},{7,6},{8,9},{9,8},{10,11... | collective-permute-start | bytes 12296 | tf_op jit(solution)/shard_map/ppermute | solution.py:333
  5.1 0.1 copy.13
  5.2 0.1 reshape.10.sel
  5.3 5.3 %forward_cosine.2 = (f32[32,16,128]{2,1,0:T(8,128)S(1)}, f32[32,16,128]{2,1,0:T(8,128)S(1)}) custom-call(s32[512]{0:T(512)S(1)} %reshape.10.sel, s32[1]{0:T(128)S(6)} %sub.3.off, bf16[128,128,128]{2,1,0:T(8,128)(2,1)} %bitcast.5, bf16[128,128,128]{2,1,0:T(8,128)(2,1)} %bitcast.9, bf16[128,128]{1,0:T(8,128)(2,1)S(1)} %copy-done.2, bf16[128,128]{1,0:T(8,128)(2,1)S(1)} %copy-done.1), custom_call_target="tpu_custom_call" | custom-call | flops 2147483648 | bytes 5242880 | tf_op jit(solution)/shard_map/forward_cosine/pallas_call | solution.py:172
  10.6 0.0 copy-start
  10.6 2.5 %collective-permute-start.1 = (f32[8,128]{1,0:T(8,128)S(1)}, f32[8,128]{1,0:T(8,128)S(1)}, u32[]{:S(2)}, u32[]{:S(2)}) collective-permute-start(f32[8,128]{1,0:T(8,128)S(1)} %add.6.first), channel_id=1, source_target_pairs={{0,2},{1,3},{2,0},{3,1},{4,6},{5,7},{6,4},{7,5},{8,10},{9,11},{10,... | collective-permute-start | bytes 12296 | tf_op jit(solution)/shard_map/ppermute | solution.py:336
  13.2 5.3 %forward_cosine.3 = (f32[32,16,128]{2,1,0:T(8,128)S(1)}, f32[32,16,128]{2,1,0:T(8,128)S(1)}) custom-call(s32[512]{0:T(512)S(1)} %reshape.10.sel, s32[1]{0:T(128)} %bitcast.off, bf16[128,128,128]{2,1,0:T(8,128)(2,1)} %bitcast.6, bf16[128,128,128]{2,1,0:T(8,128)(2,1)} %bitcast.10, bf16[128,128]{1,0:T(8,128)(2,1)S(1)} %copy-done.2, bf16[128,128]{1,0:T(8,128)(2,1)S(1)} %copy-done.1), custom_call_target="tpu_custom_call" | custom-call | flops 2147483648 | bytes 5242880 | tf_op jit(solution)/shard_map/forward_cosine/pallas_call | solution.py:172
  18.5 0.2 combine.1
  18.7 1.3 %collective-permute-start.2 = (f32[32,16,128]{2,1,0:T(8,128)S(1)}, f32[32,16,128]{2,1,0:T(8,128)S(1)}, u32[]{:S(2)}, u32[]{:S(2)}) collective-permute-start(f32[32,16,128]{2,1,0:T(8,128)S(1)} %get-tuple-element.32.refs_3_), channel_id=1, source_target_pairs={{0,4},{4,0},{8,12},{12,8},{16,20},{20,16},{24,28},{28,24},{32,36},... | collective-permute-start | bytes 786440 | tf_op jit(solution)/shard_map/ppermute | solution.py:329
  20.0 1.2 %collective-permute-done.2 = f32[32,16,128]{2,1,0:T(8,128)S(1)} collective-permute-done((f32[32,16,128]{2,1,0:T(8,128)S(1)}, f32[32,16,128]{2,1,0:T(8,128)S(1)}, u32[]{:S(2)}, u32[]{:S(2)}) %collective-permute-start.2) | collective-permute-done | bytes 262176 | tf_op jit(solution)/shard_map/ppermute | solution.py:329
  21.2 0.7 add.7
  21.9 11.2 %all-to-all-start = ((f32[32,16,128]{2,1,0:T(8,128)}), f32[32,16,128]{2,1,0:T(8,128)S(1)}, u32[]{:S(2)}, u32[]{:S(2)}) async-start(f32[32,16,128]{2,1,0:T(8,128)} %add.7), calls=%async_computation | async-start | bytes 524288 | tf_op jit(solution)/shard_map/all_to_all | solution.py:330
  33.1 7.3 %momentum_other.1.refs_7_ = bf16[128,128,128]{2,1,0:T(8,128)(2,1)} custom-call(s32[512]{0:T(512)S(1)} %reshape.10.sel, s32[1]{0:T(128)S(6)} %sub.3.off, bf16[128,128,128]{2,1,0:T(8,128)(2,1)} %bitcast.7, bf16[128,128,128]{2,1,0:T(8,128)(2,1)} %bitcast.11, f32[1,128]{1,0:T(1,128)S(1)} %get-tuple-element.28.refs_2_.refs_1_, ...), custom_call_target="tpu_custom_call" | custom-call | flops 2147483648 | bytes 6291456 | tf_op jit(solution)/shard_map/momentum_other/pallas_call | solution.py:283
  40.4 4.3 %all-to-all-done.parts = f32[32,16,128]{2,1,0:T(8,128)S(1)} async-done(((f32[32,16,128]{2,1,0:T(8,128)}), f32[32,16,128]{2,1,0:T(8,128)S(1)}, u32[]{:S(2)}, u32[]{:S(2)}) %all-to-all-start) | async-done | bytes 262176 | tf_op jit(solution)/shard_map/all_to_all | solution.py:330
  44.7 0.9 %scaled_totals.1 = f32[32,16,128]{2,1,0:T(8,128)} custom-call(f32[32,16,128]{2,1,0:T(8,128)S(1)} %all-to-all-done.parts), custom_call_target="tpu_custom_call" | custom-call | flops 1048576 | bytes 524288 | tf_op jit(solution)/shard_map/scaled_totals/pallas_call | solution.py:308
  45.6 5.0 %all-to-all-start.1 = ((f32[32,16,128]{2,1,0:T(8,128)}), f32[32,16,128]{2,1,0:T(8,128)S(1)}, u32[]{:S(2)}, u32[]{:S(2)}) async-start(f32[32,16,128]{2,1,0:T(8,128)} %scaled_totals.1), calls=%async_computation.1 | async-start | bytes 524288 | tf_op jit(solution)/shard_map/all_to_all | solution.py:330
  50.6 7.3 %momentum_own.1 = bf16[128,128,128]{2,1,0:T(8,128)(2,1)} custom-call(s32[512]{0:T(512)S(1)} %reshape.10.sel, s32[1]{0:T(128)} %bitcast.off, bf16[128,128,128]{2,1,0:T(8,128)(2,1)} %bitcast.8, bf16[128,128,128]{2,1,0:T(8,128)(2,1)} %bitcast.12, f32[1,128]{1,0:T(1,128)S(1)} %get-tuple-element.28.refs_2_.refs_1_, ...), custom_call_target="tpu_custom_call", output_to_operand_aliasing={{}: (9, {})} | custom-call | flops 2147483648 | bytes 6291456 | tf_op jit(solution)/shard_map/momentum_own/pallas_call | solution.py:283
  57.9 3.4 %all-to-all-done.1.refs_2_ = f32[32,16,128]{2,1,0:T(8,128)S(1)} async-done(((f32[32,16,128]{2,1,0:T(8,128)}), f32[32,16,128]{2,1,0:T(8,128)S(1)}, u32[]{:S(2)}, u32[]{:S(2)}) %all-to-all-start.1) | async-done | bytes 262176 | tf_op jit(solution)/shard_map/all_to_all | solution.py:330
  61.3 3.0 %collective-permute-start.3 = (f32[32,16,128]{2,1,0:T(8,128)S(1)}, f32[32,16,128]{2,1,0:T(8,128)S(1)}, u32[]{:S(2)}, u32[]{:S(2)}) collective-permute-start(f32[32,16,128]{2,1,0:T(8,128)S(1)} %all-to-all-done.1.refs_2_), channel_id=1, source_target_pairs={{0,4},{4,0},{8,12},{12,8},{16,20},{20,16},{24,28},{28,24},{32,36},... | collective-permute-start | bytes 786440 | tf_op jit(solution)/shard_map/ppermute | solution.py:329
  64.2 7.1 %weight_own.1.refs_6_ = bf16[128,128,128]{2,1,0:T(8,128)(2,1)} custom-call(s32[512]{0:T(512)S(1)} %reshape.10.sel, s32[1]{0:T(128)} %bitcast.off, bf16[128,128,128]{2,1,0:T(8,128)(2,1)} %refs_0_.3, f32[1,128]{1,0:T(1,128)S(1)} %get-tuple-element.28.refs_2_.refs_1_, f32[32,16,128]{2,1,0:T(8,128)S(1)} %all-to-all-done.1.refs_2_, ...), custom_call_target="tpu_custom_call" | custom-call | flops 2147483648 | bytes 4194304 | tf_op jit(solution)/shard_map/weight_own/pallas_call | solution.py:283
  71.3 7.1 %weight_other.1 = bf16[128,128,128]{2,1,0:T(8,128)(2,1)} custom-call(s32[512]{0:T(512)S(1)} %reshape.10.sel, s32[1]{0:T(128)S(6)} %sub.3.off, bf16[128,128,128]{2,1,0:T(8,128)(2,1)} %refs_0_.3, f32[1,128]{1,0:T(1,128)S(1)} %get-tuple-element.28.refs_2_.refs_1_, f32[32,16,128]{2,1,0:T(8,128)S(1)} %collective-permute-done.3.refs_2_, ...), custom_call_target="tpu_custom_call", output_to_operand_aliasing={{}: (8, {})} | custom-call | flops 2147483648 | bytes 4194304 | tf_op jit(solution)/shard_map/weight_other/pallas_call | solution.py:283
  (9 shorter events, 0.0 us)
Async XLA Ops:
  0.6 4.7 %copy-start.1 = (bf16[128,128]{1,0:T(8,128)(2,1)S(1)}, bf16[128,128]{1,0:T(8,128)(2,1)}, u32[]{:S(2)}) copy-start(bf16[128,128]{1,0:T(8,128)(2,1)} %constant.20.clone.t_low.refs_5_.refs_4_) | copy-start | bytes 98308
  0.6 4.7 %copy-start.2 = (bf16[128,128]{1,0:T(8,128)(2,1)S(1)}, bf16[128,128]{1,0:T(8,128)(2,1)}, u32[]{:S(2)}) copy-start(bf16[128,128]{1,0:T(8,128)(2,1)} %constant.19.clone.t_high.refs_4_.refs_3_) | copy-start | bytes 98308
  0.7 4.4 %copy-start.3 = (s32[128,4]{0,1:T(4,128)S(1)}, s32[128,4]{0,1:T(4,128)}, u32[]{:S(2)}) copy-start(s32[128,4]{0,1:T(4,128)} %param.10) | copy-start | bytes 6148
  2.9 7.7 %collective-permute-start = (f32[8,128]{1,0:T(8,128)S(1)}, f32[8,128]{1,0:T(8,128)S(1)}, u32[]{:S(2)}, u32[]{:S(2)}) collective-permute-start(f32[8,128]{1,0:T(8,128)S(1)} %square_sums.1), channel_id=1, source_target_pairs={{0,1},{1,0},{2,3},{3,2},{4,5},{5,4},{6,7},{7,6},{8,9},{9,8},{10,11... | collective-permute-start | bytes 12296 | tf_op jit(solution)/shard_map/ppermute | solution.py:333
  10.6 22.5 %copy-start = (bf16[128,384]{1,0:T(8,128)(2,1)S(1)}, bf16[128,384]{1,0:T(8,128)(2,1)}, u32[]{:S(2)}) copy-start(bf16[128,384]{1,0:T(8,128)(2,1)} %constant.21.clone.refs_6_.refs_5_) | copy-start | bytes 294916
  10.6 7.8 %collective-permute-start.1 = (f32[8,128]{1,0:T(8,128)S(1)}, f32[8,128]{1,0:T(8,128)S(1)}, u32[]{:S(2)}, u32[]{:S(2)}) collective-permute-start(f32[8,128]{1,0:T(8,128)S(1)} %add.6.first), channel_id=1, source_target_pairs={{0,2},{1,3},{2,0},{3,1},{4,6},{5,7},{6,4},{7,5},{8,10},{9,11},{10,... | collective-permute-start | bytes 12296 | tf_op jit(solution)/shard_map/ppermute | solution.py:336
  18.7 2.5 %collective-permute-start.2 = (f32[32,16,128]{2,1,0:T(8,128)S(1)}, f32[32,16,128]{2,1,0:T(8,128)S(1)}, u32[]{:S(2)}, u32[]{:S(2)}) collective-permute-start(f32[32,16,128]{2,1,0:T(8,128)S(1)} %get-tuple-element.32.refs_3_), channel_id=1, source_target_pairs={{0,4},{4,0},{8,12},{12,8},{16,20},{20,16},{24,28},{28,24},{32,36},... | collective-permute-start | bytes 786440 | tf_op jit(solution)/shard_map/ppermute | solution.py:329
  21.9 22.8 %all-to-all-start = ((f32[32,16,128]{2,1,0:T(8,128)}), f32[32,16,128]{2,1,0:T(8,128)S(1)}, u32[]{:S(2)}, u32[]{:S(2)}) async-start(f32[32,16,128]{2,1,0:T(8,128)} %add.7), calls=%async_computation | async-start | bytes 524288 | tf_op jit(solution)/shard_map/all_to_all | solution.py:330
  45.6 15.7 %all-to-all-start.1 = ((f32[32,16,128]{2,1,0:T(8,128)}), f32[32,16,128]{2,1,0:T(8,128)S(1)}, u32[]{:S(2)}, u32[]{:S(2)}) async-start(f32[32,16,128]{2,1,0:T(8,128)} %scaled_totals.1), calls=%async_computation.1 | async-start | bytes 524288 | tf_op jit(solution)/shard_map/all_to_all | solution.py:330
  61.3 10.0 %collective-permute-start.3 = (f32[32,16,128]{2,1,0:T(8,128)S(1)}, f32[32,16,128]{2,1,0:T(8,128)S(1)}, u32[]{:S(2)}, u32[]{:S(2)}) collective-permute-start(f32[32,16,128]{2,1,0:T(8,128)S(1)} %all-to-all-done.1.refs_2_), channel_id=1, source_target_pairs={{0,4},{4,0},{8,12},{12,8},{16,20},{20,16},{24,28},{28,24},{32,36},... | collective-permute-start | bytes 786440 | tf_op jit(solution)/shard_map/ppermute | solution.py:329

commit v3 on v2

--- a/solution.py
+++ b/solution.py
@@ -48,13 +48,16 @@
 
 def gather_rows(table, blocks):
     return jnp.concatenate(
-        [table[pl.ds(pl.multiple_of(b * FB, FB), FB), :] for b in blocks], axis=0
-    )
-
-
-def blocks_of(sel, pair):
-    picked = [sel[pair * 8 + q] for q in range(8)]
-    return [b // NBS for b in picked], [b % NBS for b in picked]
+        [table[pl.ds(pl.multiple_of(lax.shift_left(b, 4), FB), FB), :] for b in blocks], axis=0
+    )
+
+
+def rows_of(sel, pair):
+    return [lax.shift_right_logical(sel[pair * 8 + q], 3) for q in range(8)]
+
+
+def cols_of(sel, pair):
+    return [lax.bitwise_and(sel[pair * 8 + q], NBS - 1) for q in range(8)]
 
 
 ANY = pl.BlockSpec(memory_space=pl.ANY)
@@ -63,6 +66,7 @@
 STEP = 8
 CHUNKS = HALF // STEP
 CHUNK_GROUPS = 2 * STEP
+UNROLL = 16
 
 
 def square_kernel(g, out, buf, sem):
@@ -117,10 +121,8 @@
     return wait
 
 
-def forward_pair(g, m, rows, cols, t_high, t_low):
-    lane = lax.broadcasted_iota(jnp.int32, (FB, GROUP), 1) // FB
+def forward_rows(g, m, rows, t_high, t_low):
     row_high, row_low = gather_rows(t_high, rows), gather_rows(t_low, rows)
-    col_high, col_low = gather_rows(t_high, cols), gather_rows(t_low, cols)
     picked = []
     for s in range(2):
         own = slice(64 * s, 64 * s + 64)
@@ -128,9 +130,12 @@
         prod = dot(left, jnp.concatenate([g[s], m[s]], axis=1))
         picked.append(prod[:64] + prod[64:])
     left = jnp.concatenate(picked, axis=0)
-    left = jnp.concatenate([left[:, :GROUP], left[:, GROUP:]], axis=0)
-    high, low = split(left)
-    lhs = jnp.concatenate([high, low], axis=1)
+    return split(jnp.concatenate([left[:, :GROUP], left[:, GROUP:]], axis=0))
+
+
+def forward_cols(high, low, cols, t_high, t_low):
+    lane = lax.broadcasted_iota(jnp.int32, (FB, GROUP), 1) // FB
+    col_high, col_low = gather_rows(t_high, cols), gather_rows(t_low, cols)
     rhs = jnp.concatenate(
         [
             jnp.concatenate([col_high, col_high], axis=1),
@@ -138,7 +143,7 @@
         ],
         axis=0,
     )
-    prod = dot(lhs, rhs, NT)
+    prod = dot(jnp.concatenate([high, low], axis=1), rhs, NT)
     tiles = []
     for at in (0, GROUP):
         tile = None
@@ -158,9 +163,9 @@
         wait(c)
         for u in range(STEP):
             p = c * STEP + u
-            rows, cols = blocks_of(sel, base + p)
             pair = pl.ds(2 * p, 2)
-            cg[p], cm[p] = forward_pair(g_buf[pair], m_buf[pair], rows, cols, t_high, t_low)
+            high, low = forward_rows(g_buf[pair], m_buf[pair], rows_of(sel, base + p), t_high, t_low)
+            cg[p], cm[p] = forward_cols(high, low, cols_of(sel, base + p), t_high, t_low)
         return 0
 
     lax.fori_loop(0, CHUNKS, body, 0)
@@ -208,15 +213,27 @@
     )(first, second, *tiles)
 
 
-def decode_pair(coeffs, rows, cols, t_high, t_low, t_left):
+def place_blocks(coeffs, rows):
     lane = lax.broadcasted_iota(jnp.int32, (FB, GROUP), 1) // FB
     row_of = jnp.zeros((FB, GROUP), jnp.int32)
     for q in range(8):
         row_of = jnp.where(lane == q, rows[q], row_of)
-    parts = jnp.concatenate([jnp.where(row_of == b, coeffs, 0.0) for b in range(NBS)], axis=0)
-    high, low = split(parts)
+    high = coeffs.astype(jnp.bfloat16).astype(jnp.float32)
+    placed = []
+    for part in (high, coeffs - high):
+        parts = [jnp.where(row_of == b, part, 0.0) for b in range(NBS)]
+        placed.append(jnp.concatenate(parts, axis=0).astype(jnp.bfloat16))
+    return placed
+
+
+def decode_rows(first, second, t_left):
+    high = jnp.concatenate([first[0], second[0]], axis=1)
+    low = jnp.concatenate([first[1], second[1]], axis=1)
     left = dot(t_left[...], jnp.concatenate([high, low, high], axis=0))
-    high, low = split(left)
+    return split(left[:, :GROUP]), split(left[:, GROUP:])
+
+
+def decode_cols(high, low, cols, t_high, t_low):
     none = jnp.zeros((64, GROUP), jnp.bfloat16)
 
     def both(table):
@@ -240,9 +257,9 @@
 def decode_kernel(count, sel, off, *refs):
     arrays, refs = refs[:count], refs[count:]
     scale, coeffs, t_high, t_low, t_left = refs[:5]
-    out = refs[-(count + 4)]
-    bufs = refs[-(count + 3) : -3]
-    out_buf, sem, out_sem = refs[-3:]
+    out = refs[-(count + 6)]
+    bufs = refs[-(count + 5) : -5]
+    out_buf, high_buf, low_buf, sem, out_sem = refs[-5:]
     base = off[0] * HALF
     wait = load_half(arrays, bufs, sem, base)
 
@@ -253,20 +270,32 @@
             out_sem.at[c],
         )
 
-    def body(c, _):
-        wait(c)
-        for u in range(STEP):
-            p = c * STEP + u
-            rows, cols = blocks_of(sel, base + p)
-            for s, taken in enumerate(decode_pair(coeffs[p], rows, cols, t_high, t_low, t_left)):
+    def first(i, _):
+        for u in range(0, UNROLL, 2):
+            p = i * UNROLL + u
+            placed = [place_blocks(coeffs[p + k], rows_of(sel, base + p + k)) for k in range(2)]
+            for k, (high, low) in enumerate(decode_rows(*placed, t_left)):
+                high_buf[p + k], low_buf[p + k] = high, low
+        return 0
+
+    def second(i, _):
+        chunks = UNROLL // STEP
+        for k in range(chunks):
+            wait(i * chunks + k)
+        for u in range(UNROLL):
+            p = i * UNROLL + u
+            cols = cols_of(sel, base + p)
+            for s, taken in enumerate(decode_cols(high_buf[p], low_buf[p], cols, t_high, t_low)):
                 wide = bufs[0][2 * p + s].astype(jnp.float32)
                 if count == 2:
                     wide = momentum_retention * bufs[1][2 * p + s].astype(jnp.float32) + scale[...] * wide
                 out_buf[2 * p + s] = (wide - taken).astype(jnp.bfloat16)
-        store(c).start()
+            if (u + 1) % STEP == 0:
+                store(i * chunks + u // STEP).start()
         return 0
 
-    lax.fori_loop(0, CHUNKS, body, 0)
+    lax.fori_loop(0, HALF // UNROLL, first, 0)
+    lax.fori_loop(0, HALF // UNROLL, second, 0)
     for c in range(CHUNKS):
         store(c).wait()
 
@@ -286,6 +315,7 @@
         out_specs=ANY,
         out_shape=jax.ShapeDtypeStruct((2 * PAIRS, GROUP, GROUP), jnp.bfloat16),
         scratch_shapes=[buf] * (len(arrays) + 1)
+        + [pltpu.VMEM((HALF, GROUP, GROUP), jnp.bfloat16)] * 2
         + [pltpu.SemaphoreType.DMA((len(arrays), CHUNKS)), pltpu.SemaphoreType.DMA((CHUNKS,))],
         input_output_aliases=aliases,
         compiler_params=pltpu.CompilerParams(vmem_limit_bytes=51 << 20),

time: 78.7 us -> 72.3 us (0.919)
  Pallas kernels: 42.7 us -> 30.7 us
  waiting for transfers between devices: 8.82 us -> 14.2 us
    pallas_call x4, Pallas kernels: 28.8 us -> 17.2 us  [decode_half(): pl.pallas_call(functools.partial(decode_kernel, len(arrays)), in_specs=sp...]
    all_to_all x2, waiting for transfers between devices: 7.65 us -> 13 us  [per_device(): lax.all_to_all(x, 'rep', 0, 0, tiled=True, axis_index_groups=same_core)]
  transfers between devices with their start and end apart: 6 -> 6, of which waited for: 3 -> 3; matrix products, arithmetic and copies ran while one was open for 0% -> 0% of each run, Pallas kernels for 41% -> 32%
where the time goes in v3:
time: 72.3 us; the launch traced here: 72 us
  Pallas kernels  30.7 us (42%)
  starting transfers between devices  25.3 us (35%)
  waiting for transfers between devices  14.2 us (20%)
  between operations  0.8 us (1%)
  other arithmetic  0.74 us (1%)
    pallas_call x4, Pallas kernels, decode_half(): pl.pallas_call(functools.partial(decode_kernel, len(arrays)), in_specs=sp...  17.2 us
    all_to_all x2, starting transfers between devices, per_device(): lax.all_to_all(x, 'rep', 0, 0, tiled=True, axis_index_groups=same_core)  15.8 us
    all_to_all x2, waiting for transfers between devices, per_device(): lax.all_to_all(x, 'rep', 0, 0, tiled=True, axis_index_groups=same_core)  13 us
    pallas_call x2, Pallas kernels, forward(): pl.pallas_call(forward_kernel, in_specs=[SMEM, SMEM, ANY, ANY, VMEM, VMEM...  10.2 us
    ppermute x2, starting transfers between devices, per_device(): swap = lambda x: lax.ppermute(x, 'rep', swap_core)  4.8 us
    ppermute x1, starting transfers between devices, per_device(): far = lax.ppermute(sums, 'mdl', [(i, i ^ 2) for i in range(4)])  2.54 us
    pallas_call x1, Pallas kernels, square_sums(): pl.pallas_call(square_kernel, in_specs=[ANY], out_specs=VMEM, out_shape=j...  2.27 us
    ppermute x1, starting transfers between devices, per_device(): sums += lax.ppermute(sums, 'mdl', [(i, i ^ 1) for i in range(4)])  2.13 us
  transfers between devices with their start and end apart: 6, of which 3 were waited for; matrix products, arithmetic and copies ran while one was open for 0% of the time, Pallas kernels for 32%

profile of v3, /device:TPU:1, one launch (start us, length us, event | category | flops | bytes accessed | tf_op | source)
XLA Modules:
  0.0 72.0 jit_solution(12929741225009983216)
XLA Ops:
  0.6 0.0 copy-start.1
  0.6 0.0 copy-start.2
  0.7 2.3 %square_sums.1 = f32[8,128]{1,0:T(8,128)S(1)} custom-call(bf16[128,128,128]{2,1,0:T(8,128)(2,1)} %bitcast.4), custom_call_target="tpu_custom_call" | custom-call | flops 4194304 | bytes 4194304 | tf_op jit(solution)/shard_map/square_sums/pallas_call | solution.py:93
  2.9 2.1 %collective-permute-start = (f32[8,128]{1,0:T(8,128)S(1)}, f32[8,128]{1,0:T(8,128)S(1)}, u32[]{:S(2)}, u32[]{:S(2)}) collective-permute-start(f32[8,128]{1,0:T(8,128)S(1)} %square_sums.1), channel_id=1, source_target_pairs={{0,1},{1,0},{2,3},{3,2},{4,5},{5,4},{6,7},{7,6},{8,9},{9,8},{10,11... | collective-permute-start | bytes 12296 | tf_op jit(solution)/shard_map/ppermute | solution.py:363
  5.1 0.1 copy.13
  5.2 0.1 reshape.10.sel
  5.3 5.1 %forward_cosine.2 = (f32[32,16,128]{2,1,0:T(8,128)S(1)}, f32[32,16,128]{2,1,0:T(8,128)S(1)}) custom-call(s32[512]{0:T(512)S(1)} %reshape.10.sel, s32[1]{0:T(128)S(6)} %sub.3.off, bf16[128,128,128]{2,1,0:T(8,128)(2,1)} %bitcast.5, bf16[128,128,128]{2,1,0:T(8,128)(2,1)} %bitcast.9, bf16[128,128]{1,0:T(8,128)(2,1)S(1)} %copy-done.2, bf16[128,128]{1,0:T(8,128)(2,1)S(1)} %copy-done.1), custom_call_target="tpu_custom_call" | custom-call | flops 2147483648 | bytes 5242880 | tf_op jit(solution)/shard_map/forward_cosine/pallas_call | solution.py:177
  10.4 0.0 copy-start
  10.5 2.5 %collective-permute-start.1 = (f32[8,128]{1,0:T(8,128)S(1)}, f32[8,128]{1,0:T(8,128)S(1)}, u32[]{:S(2)}, u32[]{:S(2)}) collective-permute-start(f32[8,128]{1,0:T(8,128)S(1)} %add.6.first), channel_id=1, source_target_pairs={{0,2},{1,3},{2,0},{3,1},{4,6},{5,7},{6,4},{7,5},{8,10},{9,11},{10,... | collective-permute-start | bytes 12296 | tf_op jit(solution)/shard_map/ppermute | solution.py:366
  13.0 5.1 %forward_cosine.3 = (f32[32,16,128]{2,1,0:T(8,128)S(1)}, f32[32,16,128]{2,1,0:T(8,128)S(1)}) custom-call(s32[512]{0:T(512)S(1)} %reshape.10.sel, s32[1]{0:T(128)} %bitcast.off, bf16[128,128,128]{2,1,0:T(8,128)(2,1)} %bitcast.6, bf16[128,128,128]{2,1,0:T(8,128)(2,1)} %bitcast.10, bf16[128,128]{1,0:T(8,128)(2,1)S(1)} %copy-done.2, bf16[128,128]{1,0:T(8,128)(2,1)S(1)} %copy-done.1), custom_call_target="tpu_custom_call" | custom-call | flops 2147483648 | bytes 5242880 | tf_op jit(solution)/shard_map/forward_cosine/pallas_call | solution.py:177
  18.1 0.2 combine.1
  18.3 1.3 %collective-permute-start.2 = (f32[32,16,128]{2,1,0:T(8,128)S(1)}, f32[32,16,128]{2,1,0:T(8,128)S(1)}, u32[]{:S(2)}, u32[]{:S(2)}) collective-permute-start(f32[32,16,128]{2,1,0:T(8,128)S(1)} %get-tuple-element.32.refs_3_), channel_id=1, source_target_pairs={{0,4},{4,0},{8,12},{12,8},{16,20},{20,16},{24,28},{28,24},{32,36},... | collective-permute-start | bytes 786440 | tf_op jit(solution)/shard_map/ppermute | solution.py:359
  19.7 1.2 %collective-permute-done.2 = f32[32,16,128]{2,1,0:T(8,128)S(1)} collective-permute-done((f32[32,16,128]{2,1,0:T(8,128)S(1)}, f32[32,16,128]{2,1,0:T(8,128)S(1)}, u32[]{:S(2)}, u32[]{:S(2)}) %collective-permute-start.2) | collective-permute-done | bytes 262176 | tf_op jit(solution)/shard_map/ppermute | solution.py:359
  20.8 0.7 %add.7 = f32[32,16,128]{2,1,0:T(8,128)} add(f32[32,16,128]{2,1,0:T(8,128)S(1)} %get-tuple-element.36.refs_3_, f32[32,16,128]{2,1,0:T(8,128)S(1)} %collective-permute-done.2) | non-fusion elementwise | flops 65536 | bytes 786432 | tf_op jit(solution)/shard_map/add | solution.py:369
  21.6 11.2 %all-to-all-start = ((f32[32,16,128]{2,1,0:T(8,128)}), f32[32,16,128]{2,1,0:T(8,128)S(1)}, u32[]{:S(2)}, u32[]{:S(2)}) async-start(f32[32,16,128]{2,1,0:T(8,128)} %add.7), calls=%async_computation | async-start | bytes 524288 | tf_op jit(solution)/shard_map/all_to_all | solution.py:360
  32.8 4.5 %momentum_other.1.refs_7_ = bf16[128,128,128]{2,1,0:T(8,128)(2,1)} custom-call(s32[512]{0:T(512)S(1)} %reshape.10.sel, s32[1]{0:T(128)S(6)} %sub.3.off, bf16[128,128,128]{2,1,0:T(8,128)(2,1)} %bitcast.7, bf16[128,128,128]{2,1,0:T(8,128)(2,1)} %bitcast.11, f32[1,128]{1,0:T(1,128)S(1)} %get-tuple-element.28.refs_2_.refs_1_, ...), custom_call_target="tpu_custom_call" | custom-call | flops 2147483648 | bytes 6291456 | tf_op jit(solution)/shard_map/momentum_other/pallas_call | solution.py:312
  37.3 7.1 %all-to-all-done.parts = f32[32,16,128]{2,1,0:T(8,128)S(1)} async-done(((f32[32,16,128]{2,1,0:T(8,128)}), f32[32,16,128]{2,1,0:T(8,128)S(1)}, u32[]{:S(2)}, u32[]{:S(2)}) %all-to-all-start) | async-done | bytes 262176 | tf_op jit(solution)/shard_map/all_to_all | solution.py:360
  44.3 0.9 %scaled_totals.1 = f32[32,16,128]{2,1,0:T(8,128)} custom-call(f32[32,16,128]{2,1,0:T(8,128)S(1)} %all-to-all-done.parts), custom_call_target="tpu_custom_call" | custom-call | flops 1048576 | bytes 524288 | tf_op jit(solution)/shard_map/scaled_totals/pallas_call | solution.py:338
  45.2 4.6 %all-to-all-start.1 = ((f32[32,16,128]{2,1,0:T(8,128)}), f32[32,16,128]{2,1,0:T(8,128)S(1)}, u32[]{:S(2)}, u32[]{:S(2)}) async-start(f32[32,16,128]{2,1,0:T(8,128)} %scaled_totals.1), calls=%async_computation.1 | async-start | bytes 524288 | tf_op jit(solution)/shard_map/all_to_all | solution.py:360
  49.8 4.5 %momentum_own.1 = bf16[128,128,128]{2,1,0:T(8,128)(2,1)} custom-call(s32[512]{0:T(512)S(1)} %reshape.10.sel, s32[1]{0:T(128)} %bitcast.off, bf16[128,128,128]{2,1,0:T(8,128)(2,1)} %bitcast.8, bf16[128,128,128]{2,1,0:T(8,128)(2,1)} %bitcast.12, f32[1,128]{1,0:T(1,128)S(1)} %get-tuple-element.28.refs_2_.refs_1_, ...), custom_call_target="tpu_custom_call", output_to_operand_aliasing={{}: (9, {})} | custom-call | flops 2147483648 | bytes 6291456 | tf_op jit(solution)/shard_map/momentum_own/pallas_call | solution.py:312
  54.3 5.9 %all-to-all-done.1.refs_2_ = f32[32,16,128]{2,1,0:T(8,128)S(1)} async-done(((f32[32,16,128]{2,1,0:T(8,128)}), f32[32,16,128]{2,1,0:T(8,128)S(1)}, u32[]{:S(2)}, u32[]{:S(2)}) %all-to-all-start.1) | async-done | bytes 262176 | tf_op jit(solution)/shard_map/all_to_all | solution.py:360
  60.3 3.5 %collective-permute-start.3 = (f32[32,16,128]{2,1,0:T(8,128)S(1)}, f32[32,16,128]{2,1,0:T(8,128)S(1)}, u32[]{:S(2)}, u32[]{:S(2)}) collective-permute-start(f32[32,16,128]{2,1,0:T(8,128)S(1)} %all-to-all-done.1.refs_2_), channel_id=1, source_target_pairs={{0,4},{4,0},{8,12},{12,8},{16,20},{20,16},{24,28},{28,24},{32,36},... | collective-permute-start | bytes 786440 | tf_op jit(solution)/shard_map/ppermute | solution.py:359
  63.7 4.1 %weight_own.1.refs_6_ = bf16[128,128,128]{2,1,0:T(8,128)(2,1)} custom-call(s32[512]{0:T(512)S(1)} %reshape.10.sel, s32[1]{0:T(128)} %bitcast.off, bf16[128,128,128]{2,1,0:T(8,128)(2,1)} %refs_0_.3, f32[1,128]{1,0:T(1,128)S(1)} %get-tuple-element.28.refs_2_.refs_1_, f32[32,16,128]{2,1,0:T(8,128)S(1)} %all-to-all-done.1.refs_2_, ...), custom_call_target="tpu_custom_call" | custom-call | flops 2147483648 | bytes 4194304 | tf_op jit(solution)/shard_map/weight_own/pallas_call | solution.py:312
  67.8 4.1 %weight_other.1 = bf16[128,128,128]{2,1,0:T(8,128)(2,1)} custom-call(s32[512]{0:T(512)S(1)} %reshape.10.sel, s32[1]{0:T(128)S(6)} %sub.3.off, bf16[128,128,128]{2,1,0:T(8,128)(2,1)} %refs_0_.3, f32[1,128]{1,0:T(1,128)S(1)} %get-tuple-element.28.refs_2_.refs_1_, f32[32,16,128]{2,1,0:T(8,128)S(1)} %collective-permute-done.3.refs_2_, ...), custom_call_target="tpu_custom_call", output_to_operand_aliasing={{}: (8, {})} | custom-call | flops 2147483648 | bytes 4194304 | tf_op jit(solution)/shard_map/weight_other/pallas_call | solution.py:312
  (9 shorter events, 0.0 us)
Async XLA Ops:
  0.6 4.7 %copy-start.1 = (bf16[128,128]{1,0:T(8,128)(2,1)S(1)}, bf16[128,128]{1,0:T(8,128)(2,1)}, u32[]{:S(2)}) copy-start(bf16[128,128]{1,0:T(8,128)(2,1)} %constant.20.clone.t_low.refs_5_.refs_4_) | copy-start | bytes 98308
  0.6 4.7 %copy-start.2 = (bf16[128,128]{1,0:T(8,128)(2,1)S(1)}, bf16[128,128]{1,0:T(8,128)(2,1)}, u32[]{:S(2)}) copy-start(bf16[128,128]{1,0:T(8,128)(2,1)} %constant.19.clone.t_high.refs_4_.refs_3_) | copy-start | bytes 98308
  0.7 4.4 %copy-start.3 = (s32[128,4]{0,1:T(4,128)S(1)}, s32[128,4]{0,1:T(4,128)}, u32[]{:S(2)}) copy-start(s32[128,4]{0,1:T(4,128)} %param.10) | copy-start | bytes 6148
  2.9 7.5 %collective-permute-start = (f32[8,128]{1,0:T(8,128)S(1)}, f32[8,128]{1,0:T(8,128)S(1)}, u32[]{:S(2)}, u32[]{:S(2)}) collective-permute-start(f32[8,128]{1,0:T(8,128)S(1)} %square_sums.1), channel_id=1, source_target_pairs={{0,1},{1,0},{2,3},{3,2},{4,5},{5,4},{6,7},{7,6},{8,9},{9,8},{10,11... | collective-permute-start | bytes 12296 | tf_op jit(solution)/shard_map/ppermute | solution.py:363
  10.4 22.3 %copy-start = (bf16[128,384]{1,0:T(8,128)(2,1)S(1)}, bf16[128,384]{1,0:T(8,128)(2,1)}, u32[]{:S(2)}) copy-start(bf16[128,384]{1,0:T(8,128)(2,1)} %constant.21.clone.refs_6_.refs_5_) | copy-start | bytes 294916
  10.5 7.6 %collective-permute-start.1 = (f32[8,128]{1,0:T(8,128)S(1)}, f32[8,128]{1,0:T(8,128)S(1)}, u32[]{:S(2)}, u32[]{:S(2)}) collective-permute-start(f32[8,128]{1,0:T(8,128)S(1)} %add.6.first), channel_id=1, source_target_pairs={{0,2},{1,3},{2,0},{3,1},{4,6},{5,7},{6,4},{7,5},{8,10},{9,11},{10,... | collective-permute-start | bytes 12296 | tf_op jit(solution)/shard_map/ppermute | solution.py:366
  18.3 2.5 %collective-permute-start.2 = (f32[32,16,128]{2,1,0:T(8,128)S(1)}, f32[32,16,128]{2,1,0:T(8,128)S(1)}, u32[]{:S(2)}, u32[]{:S(2)}) collective-permute-start(f32[32,16,128]{2,1,0:T(8,128)S(1)} %get-tuple-element.32.refs_3_), channel_id=1, source_target_pairs={{0,4},{4,0},{8,12},{12,8},{16,20},{20,16},{24,28},{28,24},{32,36},... | collective-permute-start | bytes 786440 | tf_op jit(solution)/shard_map/ppermute | solution.py:359
  21.6 22.8 %all-to-all-start = ((f32[32,16,128]{2,1,0:T(8,128)}), f32[32,16,128]{2,1,0:T(8,128)S(1)}, u32[]{:S(2)}, u32[]{:S(2)}) async-start(f32[32,16,128]{2,1,0:T(8,128)} %add.7), calls=%async_computation | async-start | bytes 524288 | tf_op jit(solution)/shard_map/all_to_all | solution.py:360
  45.2 15.0 %all-to-all-start.1 = ((f32[32,16,128]{2,1,0:T(8,128)}), f32[32,16,128]{2,1,0:T(8,128)S(1)}, u32[]{:S(2)}, u32[]{:S(2)}) async-start(f32[32,16,128]{2,1,0:T(8,128)} %scaled_totals.1), calls=%async_computation.1 | async-start | bytes 524288 | tf_op jit(solution)/shard_map/all_to_all | solution.py:360
  60.3 7.6 %collective-permute-start.3 = (f32[32,16,128]{2,1,0:T(8,128)S(1)}, f32[32,16,128]{2,1,0:T(8,128)S(1)}, u32[]{:S(2)}, u32[]{:S(2)}) collective-permute-start(f32[32,16,128]{2,1,0:T(8,128)S(1)} %all-to-all-done.1.refs_2_), channel_id=1, source_target_pairs={{0,4},{4,0},{8,12},{12,8},{16,20},{20,16},{24,28},{28,24},{32,36},... | collective-permute-start | bytes 786440 | tf_op jit(solution)/shard_map/ppermute | solution.py:359

commit v4 on v3

--- a/solution.py
+++ b/solution.py
@@ -354,7 +354,7 @@
     sel = select.reshape(-1)
     own = lax.rem(lax.axis_index("rep"), 2).astype(jnp.int32).reshape(1)
     other = 1 - own
-    same_core = [list(range(c, REPS, 2)) for c in range(2)]
+    same_core = [[(c + 2 * (18 + k)) % REPS for k in range(CHIPS)] for c in range(2)]
     swap_core = [(i, i ^ 1) for i in range(REPS)]
     swap = lambda x: lax.ppermute(x, "rep", swap_core)
     exchange = lambda x: lax.all_to_all(x, "rep", 0, 0, tiled=True, axis_index_groups=same_core)

time: 72.3 us -> 67.9 us (0.939)
  waiting for transfers between devices: 14.2 us -> 4.07 us
  starting transfers between devices: 25.3 us -> 31 us
    all_to_all x2, waiting for transfers between devices: 13 us -> 2.9 us  [per_device(): lax.all_to_all(x, 'rep', 0, 0, tiled=True, axis_index_groups=same_core)]
    all_to_all x2, starting transfers between devices: 15.8 us -> 22.7 us  [per_device(): lax.all_to_all(x, 'rep', 0, 0, tiled=True, axis_index_groups=same_core)]
    ppermute x2, starting transfers between devices: 4.8 us -> 3.61 us  [per_device(): swap = lambda x: lax.ppermute(x, 'rep', swap_core)]
  transfers between devices with their start and end apart: 6 -> 6, of which waited for: 3 -> 3; matrix products, arithmetic and copies ran while one was open for 0% -> 0% of each run, Pallas kernels for 32% -> 34%
where the time goes in v4:
time: 67.9 us; the launch traced here: 67.6 us
  starting transfers between devices  31 us (46%)
  Pallas kernels  30.7 us (45%)
  waiting for transfers between devices  4.07 us (6%)
  between operations  0.8 us (1%)
  other arithmetic  0.74 us (1%)
    all_to_all x2, starting transfers between devices, per_device(): lax.all_to_all(x, 'rep', 0, 0, tiled=True, axis_index_groups=same_core)  22.7 us
    pallas_call x4, Pallas kernels, decode_half(): pl.pallas_call(functools.partial(decode_kernel, len(arrays)), in_specs=sp...  17.2 us
    pallas_call x2, Pallas kernels, forward(): pl.pallas_call(forward_kernel, in_specs=[SMEM, SMEM, ANY, ANY, VMEM, VMEM...  10.2 us
    ppermute x2, starting transfers between devices, per_device(): swap = lambda x: lax.ppermute(x, 'rep', swap_core)  3.61 us
    all_to_all x2, waiting for transfers between devices, per_device(): lax.all_to_all(x, 'rep', 0, 0, tiled=True, axis_index_groups=same_core)  2.9 us
    ppermute x1, starting transfers between devices, per_device(): far = lax.ppermute(sums, 'mdl', [(i, i ^ 2) for i in range(4)])  2.54 us
    pallas_call x1, Pallas kernels, square_sums(): pl.pallas_call(square_kernel, in_specs=[ANY], out_specs=VMEM, out_shape=j...  2.27 us
    ppermute x1, starting transfers between devices, per_device(): sums += lax.ppermute(sums, 'mdl', [(i, i ^ 1) for i in range(4)])  2.13 us
  transfers between devices with their start and end apart: 6, of which 3 were waited for; matrix products, arithmetic and copies ran while one was open for 0% of the time, Pallas kernels for 34%

profile of v4, /device:TPU:1, one launch (start us, length us, event | category | flops | bytes accessed | tf_op | source)
XLA Modules:
  0.0 67.6 jit_solution(7168154786841251039)
XLA Ops:
  0.6 0.0 copy-start.1
  0.6 0.0 copy-start.2
  0.7 2.3 %square_sums.1 = f32[8,128]{1,0:T(8,128)S(1)} custom-call(bf16[128,128,128]{2,1,0:T(8,128)(2,1)} %bitcast.4), custom_call_target="tpu_custom_call" | custom-call | flops 4194304 | bytes 4194304 | tf_op jit(solution)/shard_map/square_sums/pallas_call | solution.py:93
  2.9 2.1 %collective-permute-start = (f32[8,128]{1,0:T(8,128)S(1)}, f32[8,128]{1,0:T(8,128)S(1)}, u32[]{:S(2)}, u32[]{:S(2)}) collective-permute-start(f32[8,128]{1,0:T(8,128)S(1)} %square_sums.1), channel_id=1, source_target_pairs={{0,1},{1,0},{2,3},{3,2},{4,5},{5,4},{6,7},{7,6},{8,9},{9,8},{10,11... | collective-permute-start | bytes 12296 | tf_op jit(solution)/shard_map/ppermute | solution.py:363
  5.1 0.1 copy.13
  5.2 0.1 reshape.10.sel
  5.3 5.1 %forward_cosine.2 = (f32[32,16,128]{2,1,0:T(8,128)S(1)}, f32[32,16,128]{2,1,0:T(8,128)S(1)}) custom-call(s32[512]{0:T(512)S(1)} %reshape.10.sel, s32[1]{0:T(128)S(6)} %sub.3.off, bf16[128,128,128]{2,1,0:T(8,128)(2,1)} %bitcast.5, bf16[128,128,128]{2,1,0:T(8,128)(2,1)} %bitcast.9, bf16[128,128]{1,0:T(8,128)(2,1)S(1)} %copy-done.2, bf16[128,128]{1,0:T(8,128)(2,1)S(1)} %copy-done.1), custom_call_target="tpu_custom_call" | custom-call | flops 2147483648 | bytes 5242880 | tf_op jit(solution)/shard_map/forward_cosine/pallas_call | solution.py:177
  10.4 0.0 copy-start
  10.4 2.5 %collective-permute-start.1 = (f32[8,128]{1,0:T(8,128)S(1)}, f32[8,128]{1,0:T(8,128)S(1)}, u32[]{:S(2)}, u32[]{:S(2)}) collective-permute-start(f32[8,128]{1,0:T(8,128)S(1)} %add.6.first), channel_id=1, source_target_pairs={{0,2},{1,3},{2,0},{3,1},{4,6},{5,7},{6,4},{7,5},{8,10},{9,11},{10,... | collective-permute-start | bytes 12296 | tf_op jit(solution)/shard_map/ppermute | solution.py:366
  13.0 5.1 %forward_cosine.3 = (f32[32,16,128]{2,1,0:T(8,128)S(1)}, f32[32,16,128]{2,1,0:T(8,128)S(1)}) custom-call(s32[512]{0:T(512)S(1)} %reshape.10.sel, s32[1]{0:T(128)} %bitcast.off, bf16[128,128,128]{2,1,0:T(8,128)(2,1)} %bitcast.6, bf16[128,128,128]{2,1,0:T(8,128)(2,1)} %bitcast.10, bf16[128,128]{1,0:T(8,128)(2,1)S(1)} %copy-done.2, bf16[128,128]{1,0:T(8,128)(2,1)S(1)} %copy-done.1), custom_call_target="tpu_custom_call" | custom-call | flops 2147483648 | bytes 5242880 | tf_op jit(solution)/shard_map/forward_cosine/pallas_call | solution.py:177
  18.1 0.2 combine.1
  18.3 1.3 %collective-permute-start.2 = (f32[32,16,128]{2,1,0:T(8,128)S(1)}, f32[32,16,128]{2,1,0:T(8,128)S(1)}, u32[]{:S(2)}, u32[]{:S(2)}) collective-permute-start(f32[32,16,128]{2,1,0:T(8,128)S(1)} %get-tuple-element.32.refs_3_), channel_id=1, source_target_pairs={{0,4},{4,0},{8,12},{12,8},{16,20},{20,16},{24,28},{28,24},{32,36},... | collective-permute-start | bytes 786440 | tf_op jit(solution)/shard_map/ppermute | solution.py:359
  19.6 1.2 %collective-permute-done.2 = f32[32,16,128]{2,1,0:T(8,128)S(1)} collective-permute-done((f32[32,16,128]{2,1,0:T(8,128)S(1)}, f32[32,16,128]{2,1,0:T(8,128)S(1)}, u32[]{:S(2)}, u32[]{:S(2)}) %collective-permute-start.2) | collective-permute-done | bytes 262176 | tf_op jit(solution)/shard_map/ppermute | solution.py:359
  20.8 0.7 %add.7 = f32[32,16,128]{2,1,0:T(8,128)} add(f32[32,16,128]{2,1,0:T(8,128)S(1)} %get-tuple-element.36.refs_3_, f32[32,16,128]{2,1,0:T(8,128)S(1)} %collective-permute-done.2) | non-fusion elementwise | flops 65536 | bytes 786432 | tf_op jit(solution)/shard_map/add | solution.py:369
  21.5 13.3 %all-to-all-start = ((f32[32,16,128]{2,1,0:T(8,128)}), f32[32,16,128]{2,1,0:T(8,128)S(1)}, u32[]{:S(2)}, u32[]{:S(2)}) async-start(f32[32,16,128]{2,1,0:T(8,128)} %add.7), calls=%async_computation | async-start | bytes 524288 | tf_op jit(solution)/shard_map/all_to_all | solution.py:360
  34.9 4.5 %momentum_other.1.refs_7_ = bf16[128,128,128]{2,1,0:T(8,128)(2,1)} custom-call(s32[512]{0:T(512)S(1)} %reshape.10.sel, s32[1]{0:T(128)S(6)} %sub.3.off, bf16[128,128,128]{2,1,0:T(8,128)(2,1)} %bitcast.7, bf16[128,128,128]{2,1,0:T(8,128)(2,1)} %bitcast.11, f32[1,128]{1,0:T(1,128)S(1)} %get-tuple-element.28.refs_2_.refs_1_, ...), custom_call_target="tpu_custom_call" | custom-call | flops 2147483648 | bytes 6291456 | tf_op jit(solution)/shard_map/momentum_other/pallas_call | solution.py:312
  39.4 2.1 %all-to-all-done.parts = f32[32,16,128]{2,1,0:T(8,128)S(1)} async-done(((f32[32,16,128]{2,1,0:T(8,128)}), f32[32,16,128]{2,1,0:T(8,128)S(1)}, u32[]{:S(2)}, u32[]{:S(2)}) %all-to-all-start) | async-done | bytes 262176 | tf_op jit(solution)/shard_map/all_to_all | solution.py:360
  41.5 0.9 %scaled_totals.1 = f32[32,16,128]{2,1,0:T(8,128)} custom-call(f32[32,16,128]{2,1,0:T(8,128)S(1)} %all-to-all-done.parts), custom_call_target="tpu_custom_call" | custom-call | flops 1048576 | bytes 524288 | tf_op jit(solution)/shard_map/scaled_totals/pallas_call | solution.py:338
  42.4 9.4 %all-to-all-start.1 = ((f32[32,16,128]{2,1,0:T(8,128)}), f32[32,16,128]{2,1,0:T(8,128)S(1)}, u32[]{:S(2)}, u32[]{:S(2)}) async-start(f32[32,16,128]{2,1,0:T(8,128)} %scaled_totals.1), calls=%async_computation.1 | async-start | bytes 524288 | tf_op jit(solution)/shard_map/all_to_all | solution.py:360
  51.8 4.5 %momentum_own.1 = bf16[128,128,128]{2,1,0:T(8,128)(2,1)} custom-call(s32[512]{0:T(512)S(1)} %reshape.10.sel, s32[1]{0:T(128)} %bitcast.off, bf16[128,128,128]{2,1,0:T(8,128)(2,1)} %bitcast.8, bf16[128,128,128]{2,1,0:T(8,128)(2,1)} %bitcast.12, f32[1,128]{1,0:T(1,128)S(1)} %get-tuple-element.28.refs_2_.refs_1_, ...), custom_call_target="tpu_custom_call", output_to_operand_aliasing={{}: (9, {})} | custom-call | flops 2147483648 | bytes 6291456 | tf_op jit(solution)/shard_map/momentum_own/pallas_call | solution.py:312
  56.3 0.8 %all-to-all-done.1.refs_2_ = f32[32,16,128]{2,1,0:T(8,128)S(1)} async-done(((f32[32,16,128]{2,1,0:T(8,128)}), f32[32,16,128]{2,1,0:T(8,128)S(1)}, u32[]{:S(2)}, u32[]{:S(2)}) %all-to-all-start.1) | async-done | bytes 262176 | tf_op jit(solution)/shard_map/all_to_all | solution.py:360
  57.1 2.3 %collective-permute-start.3 = (f32[32,16,128]{2,1,0:T(8,128)S(1)}, f32[32,16,128]{2,1,0:T(8,128)S(1)}, u32[]{:S(2)}, u32[]{:S(2)}) collective-permute-start(f32[32,16,128]{2,1,0:T(8,128)S(1)} %all-to-all-done.1.refs_2_), channel_id=1, source_target_pairs={{0,4},{4,0},{8,12},{12,8},{16,20},{20,16},{24,28},{28,24},{32,36},... | collective-permute-start | bytes 786440 | tf_op jit(solution)/shard_map/ppermute | solution.py:359
  59.3 4.1 %weight_own.1.refs_6_ = bf16[128,128,128]{2,1,0:T(8,128)(2,1)} custom-call(s32[512]{0:T(512)S(1)} %reshape.10.sel, s32[1]{0:T(128)} %bitcast.off, bf16[128,128,128]{2,1,0:T(8,128)(2,1)} %refs_0_.3, f32[1,128]{1,0:T(1,128)S(1)} %get-tuple-element.28.refs_2_.refs_1_, f32[32,16,128]{2,1,0:T(8,128)S(1)} %all-to-all-done.1.refs_2_, ...), custom_call_target="tpu_custom_call" | custom-call | flops 2147483648 | bytes 4194304 | tf_op jit(solution)/shard_map/weight_own/pallas_call | solution.py:312
  63.5 4.1 %weight_other.1 = bf16[128,128,128]{2,1,0:T(8,128)(2,1)} custom-call(s32[512]{0:T(512)S(1)} %reshape.10.sel, s32[1]{0:T(128)S(6)} %sub.3.off, bf16[128,128,128]{2,1,0:T(8,128)(2,1)} %refs_0_.3, f32[1,128]{1,0:T(1,128)S(1)} %get-tuple-element.28.refs_2_.refs_1_, f32[32,16,128]{2,1,0:T(8,128)S(1)} %collective-permute-done.3.refs_2_, ...), custom_call_target="tpu_custom_call", output_to_operand_aliasing={{}: (8, {})} | custom-call | flops 2147483648 | bytes 4194304 | tf_op jit(solution)/shard_map/weight_other/pallas_call | solution.py:312
  (9 shorter events, 0.0 us)
Async XLA Ops:
  0.6 4.7 %copy-start.1 = (bf16[128,128]{1,0:T(8,128)(2,1)S(1)}, bf16[128,128]{1,0:T(8,128)(2,1)}, u32[]{:S(2)}) copy-start(bf16[128,128]{1,0:T(8,128)(2,1)} %constant.20.clone.t_low.refs_5_.refs_4_) | copy-start | bytes 98308
  0.6 4.7 %copy-start.2 = (bf16[128,128]{1,0:T(8,128)(2,1)S(1)}, bf16[128,128]{1,0:T(8,128)(2,1)}, u32[]{:S(2)}) copy-start(bf16[128,128]{1,0:T(8,128)(2,1)} %constant.19.clone.t_high.refs_4_.refs_3_) | copy-start | bytes 98308
  0.7 4.4 %copy-start.3 = (s32[128,4]{0,1:T(4,128)S(1)}, s32[128,4]{0,1:T(4,128)}, u32[]{:S(2)}) copy-start(s32[128,4]{0,1:T(4,128)} %param.10) | copy-start | bytes 6148
  2.9 7.5 %collective-permute-start = (f32[8,128]{1,0:T(8,128)S(1)}, f32[8,128]{1,0:T(8,128)S(1)}, u32[]{:S(2)}, u32[]{:S(2)}) collective-permute-start(f32[8,128]{1,0:T(8,128)S(1)} %square_sums.1), channel_id=1, source_target_pairs={{0,1},{1,0},{2,3},{3,2},{4,5},{5,4},{6,7},{7,6},{8,9},{9,8},{10,11... | collective-permute-start | bytes 12296 | tf_op jit(solution)/shard_map/ppermute | solution.py:363
  10.4 24.5 %copy-start = (bf16[128,384]{1,0:T(8,128)(2,1)S(1)}, bf16[128,384]{1,0:T(8,128)(2,1)}, u32[]{:S(2)}) copy-start(bf16[128,384]{1,0:T(8,128)(2,1)} %constant.21.clone.refs_6_.refs_5_) | copy-start | bytes 294916
  10.4 7.6 %collective-permute-start.1 = (f32[8,128]{1,0:T(8,128)S(1)}, f32[8,128]{1,0:T(8,128)S(1)}, u32[]{:S(2)}, u32[]{:S(2)}) collective-permute-start(f32[8,128]{1,0:T(8,128)S(1)} %add.6.first), channel_id=1, source_target_pairs={{0,2},{1,3},{2,0},{3,1},{4,6},{5,7},{6,4},{7,5},{8,10},{9,11},{10,... | collective-permute-start | bytes 12296 | tf_op jit(solution)/shard_map/ppermute | solution.py:366
  18.3 2.5 %collective-permute-start.2 = (f32[32,16,128]{2,1,0:T(8,128)S(1)}, f32[32,16,128]{2,1,0:T(8,128)S(1)}, u32[]{:S(2)}, u32[]{:S(2)}) collective-permute-start(f32[32,16,128]{2,1,0:T(8,128)S(1)} %get-tuple-element.32.refs_3_), channel_id=1, source_target_pairs={{0,4},{4,0},{8,12},{12,8},{16,20},{20,16},{24,28},{28,24},{32,36},... | collective-permute-start | bytes 786440 | tf_op jit(solution)/shard_map/ppermute | solution.py:359
  21.5 20.0 %all-to-all-start = ((f32[32,16,128]{2,1,0:T(8,128)}), f32[32,16,128]{2,1,0:T(8,128)S(1)}, u32[]{:S(2)}, u32[]{:S(2)}) async-start(f32[32,16,128]{2,1,0:T(8,128)} %add.7), calls=%async_computation | async-start | bytes 524288 | tf_op jit(solution)/shard_map/all_to_all | solution.py:360
  42.4 14.7 %all-to-all-start.1 = ((f32[32,16,128]{2,1,0:T(8,128)}), f32[32,16,128]{2,1,0:T(8,128)S(1)}, u32[]{:S(2)}, u32[]{:S(2)}) async-start(f32[32,16,128]{2,1,0:T(8,128)} %scaled_totals.1), calls=%async_computation.1 | async-start | bytes 524288 | tf_op jit(solution)/shard_map/all_to_all | solution.py:360
  57.1 6.4 %collective-permute-start.3 = (f32[32,16,128]{2,1,0:T(8,128)S(1)}, f32[32,16,128]{2,1,0:T(8,128)S(1)}, u32[]{:S(2)}, u32[]{:S(2)}) collective-permute-start(f32[32,16,128]{2,1,0:T(8,128)S(1)} %all-to-all-done.1.refs_2_), channel_id=1, source_target_pairs={{0,4},{4,0},{8,12},{12,8},{16,20},{20,16},{24,28},{28,24},{32,36},... | collective-permute-start | bytes 786440 | tf_op jit(solution)/shard_map/ppermute | solution.py:359

commit v5 on v4

--- a/solution.py
+++ b/solution.py
@@ -102,6 +102,11 @@
     )(grads)
 
 
+def half_base(swapped):
+    core = lax.rem(lax.axis_index("rep"), 2)
+    return (1 - core if swapped else core) * HALF
+
+
 def load_half(arrays, bufs, sem, base):
     def load(a, c):
         return pltpu.make_async_copy(
@@ -133,57 +138,72 @@
     return split(jnp.concatenate([left[:, :GROUP], left[:, GROUP:]], axis=0))
 
 
-def forward_cols(high, low, cols, t_high, t_low):
+def forward_cols(highs, lows, cols, t_right):
     lane = lax.broadcasted_iota(jnp.int32, (FB, GROUP), 1) // FB
-    col_high, col_low = gather_rows(t_high, cols), gather_rows(t_low, cols)
-    rhs = jnp.concatenate(
-        [
-            jnp.concatenate([col_high, col_high], axis=1),
-            jnp.concatenate([col_low, jnp.zeros_like(col_low)], axis=1),
-        ],
-        axis=0,
-    )
-    prod = dot(jnp.concatenate([high, low], axis=1), rhs, NT)
-    tiles = []
-    for at in (0, GROUP):
-        tile = None
-        for q in range(8):
-            part = prod[at + FB * q : at + FB * q + FB]
-            part = part[:, :GROUP] + part[:, GROUP:]
-            tile = part if q == 0 else jnp.where(lane == q, part, tile)
-        tiles.append(tile)
-    return tiles
-
-
-def forward_kernel(sel, off, g, m, t_high, t_low, cg, cm, g_buf, m_buf, sem):
-    base = off[0] * HALF
+    lhs = jnp.concatenate([jnp.concatenate(highs, axis=0), jnp.concatenate(lows, axis=0)], axis=1)
+    prod = dot(lhs, t_right[...])
+    prod = prod[:, :GROUP] + prod[:, GROUP:]
+    result = []
+    for k, col in enumerate(cols):
+        tiles = []
+        for at in (2 * k * GROUP, (2 * k + 1) * GROUP):
+            tile = None
+            for q in range(8):
+                shift = lax.bitwise_and(FB * q - lax.shift_left(col[q], 4), GROUP - 1)
+                part = pltpu.roll(prod[at + FB * q : at + FB * q + FB], shift, 1)
+                tile = part if q == 0 else jnp.where(lane == q, part, tile)
+            tiles.append(tile)
+        result.append(tiles)
+    return result
+
+
+def forward_kernel(swapped, sel_in, g, m, t_high, t_low, t_right, cg, cm, g_buf, m_buf, sel, sem, sel_sem):
+    base = half_base(swapped)
+    picked = pltpu.make_async_copy(sel_in, sel, sel_sem)
+    picked.start()
     wait = load_half((g, m), (g_buf, m_buf), sem, base)
-
-    def body(c, _):
-        wait(c)
-        for u in range(STEP):
-            p = c * STEP + u
+    picked.wait()
+
+    def body(i, _):
+        highs, lows = [], []
+        for u in range(UNROLL):
+            p = i * UNROLL + u
+            if u % STEP == 0:
+                wait(i * (UNROLL // STEP) + u // STEP)
             pair = pl.ds(2 * p, 2)
             high, low = forward_rows(g_buf[pair], m_buf[pair], rows_of(sel, base + p), t_high, t_low)
-            cg[p], cm[p] = forward_cols(high, low, cols_of(sel, base + p), t_high, t_low)
+            highs.append(high)
+            lows.append(low)
+        for u in range(0, UNROLL, 2):
+            p = i * UNROLL + u
+            cols = [cols_of(sel, base + p + k) for k in range(2)]
+            tiles = forward_cols(highs[u : u + 2], lows[u : u + 2], cols, t_right)
+            for k in range(2):
+                cg[p + k], cm[p + k] = tiles[k]
         return 0
 
-    lax.fori_loop(0, CHUNKS, body, 0)
-
-
-def forward(sel, half, grads, momentum, t_high, t_low):
+    lax.fori_loop(0, HALF // UNROLL, body, 0)
+
+
+def forward(sel, swapped, grads, momentum, *tables):
     shape = jax.ShapeDtypeStruct((HALF, FB, GROUP), jnp.float32)
     buf = pltpu.VMEM((2 * HALF, GROUP, GROUP), jnp.bfloat16)
     return pl.pallas_call(
-        forward_kernel,
-        in_specs=[SMEM, SMEM, ANY, ANY, VMEM, VMEM],
+        functools.partial(forward_kernel, swapped),
+        in_specs=[ANY] * 3 + [VMEM] * 3,
         out_specs=[VMEM, VMEM],
         out_shape=[shape, shape],
-        scratch_shapes=[buf, buf, pltpu.SemaphoreType.DMA((2, CHUNKS))],
+        scratch_shapes=[
+            buf,
+            buf,
+            pltpu.SMEM((2 * PAIRS * KSEL,), jnp.int32),
+            pltpu.SemaphoreType.DMA((2, CHUNKS)),
+            pltpu.SemaphoreType.DMA,
+        ],
         compiler_params=pltpu.CompilerParams(vmem_limit_bytes=51 << 20),
         cost_estimate=pl.CostEstimate(flops=2 << 30, bytes_accessed=5 << 20, transcendentals=0),
         name="forward_cosine",
-    )(sel, half, grads, momentum, t_high, t_low)
+    )(sel, grads, momentum, *tables)
 
 
 def clip_of(first, second):
@@ -213,11 +233,8 @@
     )(first, second, *tiles)
 
 
-def place_blocks(coeffs, rows):
-    lane = lax.broadcasted_iota(jnp.int32, (FB, GROUP), 1) // FB
-    row_of = jnp.zeros((FB, GROUP), jnp.int32)
-    for q in range(8):
-        row_of = jnp.where(lane == q, rows[q], row_of)
+def place_blocks(coeffs, row_of):
+    row_of = jnp.broadcast_to(row_of, coeffs.shape)
     high = coeffs.astype(jnp.bfloat16).astype(jnp.float32)
     placed = []
     for part in (high, coeffs - high):
@@ -254,13 +271,15 @@
     return result[:, :GROUP], result[:, GROUP:]
 
 
-def decode_kernel(count, sel, off, *refs):
+def decode_kernel(count, swapped, sel_in, *refs):
     arrays, refs = refs[:count], refs[count:]
-    scale, coeffs, t_high, t_low, t_left = refs[:5]
-    out = refs[-(count + 6)]
-    bufs = refs[-(count + 5) : -5]
-    out_buf, high_buf, low_buf, sem, out_sem = refs[-5:]
-    base = off[0] * HALF
+    scale, coeffs, row_of, t_high, t_low, t_left = refs[:6]
+    out = refs[-(count + 8)]
+    bufs = refs[-(count + 7) : -7]
+    out_buf, high_buf, low_buf, sel, sem, out_sem, sel_sem = refs[-7:]
+    base = half_base(swapped)
+    picked = pltpu.make_async_copy(sel_in, sel, sel_sem)
+    picked.start()
     wait = load_half(arrays, bufs, sem, base)
 
     def store(c):
@@ -273,7 +292,7 @@
     def first(i, _):
         for u in range(0, UNROLL, 2):
             p = i * UNROLL + u
-            placed = [place_blocks(coeffs[p + k], rows_of(sel, base + p + k)) for k in range(2)]
+            placed = [place_blocks(coeffs[p + k], row_of[pl.ds(base + p + k, 1)]) for k in range(2)]
             for k, (high, low) in enumerate(decode_rows(*placed, t_left)):
                 high_buf[p + k], low_buf[p + k] = high, low
         return 0
@@ -295,14 +314,15 @@
         return 0
 
     lax.fori_loop(0, HALF // UNROLL, first, 0)
+    picked.wait()
     lax.fori_loop(0, HALF // UNROLL, second, 0)
     for c in range(CHUNKS):
         store(c).wait()
 
 
-def decode_half(sel, half, arrays, scale, coeffs, tables, before, name):
-    operands = (sel, half, *arrays, scale, coeffs, *tables)
-    specs = [SMEM, SMEM] + [ANY] * len(arrays) + [VMEM] * 5
+def decode_half(sel, swapped, arrays, scale, coeffs, row_of, tables, before, name):
+    operands = (sel, *arrays, scale, coeffs, row_of, *tables)
+    specs = [ANY] + [ANY] * len(arrays) + [VMEM] * 6
     aliases = {}
     if before is not None:
         aliases = {len(operands): 0}
@@ -310,13 +330,18 @@
         specs.append(ANY)
     buf = pltpu.VMEM((2 * HALF, GROUP, GROUP), jnp.bfloat16)
     return pl.pallas_call(
-        functools.partial(decode_kernel, len(arrays)),
+        functools.partial(decode_kernel, len(arrays), swapped),
         in_specs=specs,
         out_specs=ANY,
         out_shape=jax.ShapeDtypeStruct((2 * PAIRS, GROUP, GROUP), jnp.bfloat16),
         scratch_shapes=[buf] * (len(arrays) + 1)
         + [pltpu.VMEM((HALF, GROUP, GROUP), jnp.bfloat16)] * 2
-        + [pltpu.SemaphoreType.DMA((len(arrays), CHUNKS)), pltpu.SemaphoreType.DMA((CHUNKS,))],
+        + [
+            pltpu.SMEM((2 * PAIRS * KSEL,), jnp.int32),
+            pltpu.SemaphoreType.DMA((len(arrays), CHUNKS)),
+            pltpu.SemaphoreType.DMA((CHUNKS,)),
+            pltpu.SemaphoreType.DMA,
+        ],
         input_output_aliases=aliases,
         compiler_params=pltpu.CompilerParams(vmem_limit_bytes=51 << 20),
         cost_estimate=pl.CostEstimate(flops=2 << 30, bytes_accessed=(2 << 20) * (1 + len(arrays)), transcendentals=0),
@@ -349,11 +374,11 @@
 def per_device(grads, momentum, weight, select):
     high, low = dct_tables()
     left = np.concatenate([high.T, high.T, low.T], axis=1)
+    right = np.concatenate([high.T, low.T, high.T, np.zeros_like(low)], axis=1)
+    t_right = jnp.asarray(np.concatenate([right[:, : 2 * GROUP], right[:, 2 * GROUP :]], axis=0))
     t_high, t_low, t_left = tables = tuple(jnp.asarray(table) for table in (high, low, left))
     grads, momentum = grads[0], momentum[0]
     sel = select.reshape(-1)
-    own = lax.rem(lax.axis_index("rep"), 2).astype(jnp.int32).reshape(1)
-    other = 1 - own
     same_core = [[(c + 2 * (18 + k)) % REPS for k in range(CHIPS)] for c in range(2)]
     swap_core = [(i, i ^ 1) for i in range(REPS)]
     swap = lambda x: lax.ppermute(x, "rep", swap_core)
@@ -361,27 +386,29 @@
 
     sums = square_sums(grads)
     sums += lax.ppermute(sums, "mdl", [(i, i ^ 1) for i in range(4)])
-    g_other, m_other = forward(sel, other, grads, momentum, t_high, t_low)
+    g_other, m_other = forward(sel, True, grads, momentum, t_high, t_low, t_right)
     sums, g_other, m_other = lax.optimization_barrier((sums, g_other, m_other))
     far = lax.ppermute(sums, "mdl", [(i, i ^ 2) for i in range(4)])
-    g_own, m_own = forward(sel, own, grads, momentum, t_high, t_low)
+    g_own, m_own = forward(sel, False, grads, momentum, t_high, t_low, t_right)
     c_other, c_own, clip = combine(sums, far, g_other, m_other, g_own, m_own)
     chip, c_other, c_own = lax.optimization_barrier((c_own + swap(c_other), c_other, c_own))
+    select, _ = lax.optimization_barrier((select, chip))
+    row_of = jnp.repeat(lax.shift_right_logical(select, 3), FB, axis=1).reshape(PAIRS, GROUP)
     parts = exchange(chip)
     new_momentum = decode_half(
-        sel, other, (grads, momentum), clip, c_other, tables, None, "momentum_other"
+        sel, True, (grads, momentum), clip, c_other, row_of, tables, None, "momentum_other"
     )
     parts, new_momentum = lax.optimization_barrier((parts, new_momentum))
     mine, c_own = lax.optimization_barrier((scaled_totals(parts), c_own))
     totals_own = exchange(mine)
     new_momentum = decode_half(
-        sel, own, (grads, momentum), clip, c_own, tables, new_momentum, "momentum_own"
+        sel, False, (grads, momentum), clip, c_own, row_of, tables, new_momentum, "momentum_own"
     )
     totals_own, new_momentum = lax.optimization_barrier((totals_own, new_momentum))
     totals_other = swap(totals_own)
-    new_weight = decode_half(sel, own, (weight,), clip, totals_own, tables, None, "weight_own")
+    new_weight = decode_half(sel, False, (weight,), clip, totals_own, row_of, tables, None, "weight_own")
     new_weight = decode_half(
-        sel, other, (weight,), clip, totals_other, tables, new_weight, "weight_other"
+        sel, True, (weight,), clip, totals_other, row_of, tables, new_weight, "weight_other"
     )
     return (new_weight, new_momentum[None])
 

time: 67.9 us -> 65.1 us (0.959)
  Pallas kernels: 30.7 us -> 26.8 us
    pallas_call x6, Pallas kernels: 27.4 us -> 23.4 us  [the longest x4 14.9 us: decode_half(): pl.pallas_call(functools.partial(decode_kernel, len(arrays), swapped), in...]
  transfers between devices with their start and end apart: 6 -> 6, of which waited for: 3 -> 3; matrix products, arithmetic and copies ran while one was open for 0% -> 1% of each run, Pallas kernels for 34% -> 31%
where the time goes in v5:
time: 65.1 us; the launch traced here: 64.8 us
  starting transfers between devices  31 us (48%)
  Pallas kernels  26.8 us (41%)
  waiting for transfers between devices  4.68 us (7%)
  between operations  0.82 us (1%)
  local copies, waits for them, and re-layouts  0.75 us (1%)
  other arithmetic  0.74 us (1%)
    all_to_all x2, starting transfers between devices, per_device(): lax.all_to_all(x, 'rep', 0, 0, tiled=True, axis_index_groups=same_core)  22.7 us
    pallas_call x4, Pallas kernels, decode_half(): pl.pallas_call(functools.partial(decode_kernel, len(arrays), swapped), in...  14.9 us
    pallas_call x2, Pallas kernels, forward(): pl.pallas_call(functools.partial(forward_kernel, swapped), in_specs=[ANY]...  8.5 us
    ppermute x2, starting transfers between devices, per_device(): swap = lambda x: lax.ppermute(x, 'rep', swap_core)  3.61 us
    all_to_all x2, waiting for transfers between devices, per_device(): lax.all_to_all(x, 'rep', 0, 0, tiled=True, axis_index_groups=same_core)  3.51 us
    ppermute x1, starting transfers between devices, per_device(): far = lax.ppermute(sums, 'mdl', [(i, i ^ 2) for i in range(4)])  2.53 us
    pallas_call x1, Pallas kernels, square_sums(): pl.pallas_call(square_kernel, in_specs=[ANY], out_specs=VMEM, out_shape=j...  2.29 us
    ppermute x1, starting transfers between devices, per_device(): sums += lax.ppermute(sums, 'mdl', [(i, i ^ 1) for i in range(4)])  2.13 us
  transfers between devices with their start and end apart: 6, of which 3 were waited for; matrix products, arithmetic and copies ran while one was open for 1% of the time, Pallas kernels for 31%

profile of v5, /device:TPU:1, one launch (start us, length us, event | category | flops | bytes accessed | tf_op | source)
XLA Modules:
  0.0 64.8 jit_solution(13879000182335299)
XLA Ops:
  0.7 2.3 %square_sums.1 = f32[8,128]{1,0:T(8,128)S(1)} custom-call(bf16[128,128,128]{2,1,0:T(8,128)(2,1)} %bitcast.3), custom_call_target="tpu_custom_call" | custom-call | flops 4194304 | bytes 4194304 | tf_op jit(solution)/shard_map/square_sums/pallas_call | solution.py:93
  3.0 2.1 %collective-permute-start = (f32[8,128]{1,0:T(8,128)S(1)}, f32[8,128]{1,0:T(8,128)S(1)}, u32[]{:S(2)}, u32[]{:S(2)}) collective-permute-start(f32[8,128]{1,0:T(8,128)S(1)} %square_sums.1), channel_id=1, source_target_pairs={{0,1},{1,0},{2,3},{3,2},{4,5},{5,4},{6,7},{7,6},{8,9},{9,8},{10,11... | collective-permute-start | bytes 12296 | tf_op jit(solution)/shard_map/ppermute | solution.py:388
  5.1 0.1 copy.15
  5.2 0.1 reshape.7.sel_in
  5.4 4.3 %forward_cosine.2 = (f32[32,16,128]{2,1,0:T(8,128)S(1)}, f32[32,16,128]{2,1,0:T(8,128)S(1)}) custom-call(s32[512]{0:T(512)S(1)} %reshape.7.sel_in, bf16[128,128,128]{2,1,0:T(8,128)(2,1)} %bitcast.4, bf16[128,128,128]{2,1,0:T(8,128)(2,1)} %bitcast.8, bf16[128,128]{1,0:T(8,128)(2,1)S(1)} %copy-done.2, bf16[128,128]{1,0:T(8,128)(2,1)S(1)} %copy-done.1, ...), custom_call_target="tpu_custom_call" | custom-call | flops 2147483648 | bytes 5242880 | tf_op jit(solution)/shard_map/forward_cosine/pallas_call | solution.py:191
  9.7 2.5 %collective-permute-start.1 = (f32[8,128]{1,0:T(8,128)S(1)}, f32[8,128]{1,0:T(8,128)S(1)}, u32[]{:S(2)}, u32[]{:S(2)}) collective-permute-start(f32[8,128]{1,0:T(8,128)S(1)} %add.6.first), channel_id=1, source_target_pairs={{0,2},{1,3},{2,0},{3,1},{4,6},{5,7},{6,4},{7,5},{8,10},{9,11},{10,... | collective-permute-start | bytes 12296 | tf_op jit(solution)/shard_map/ppermute | solution.py:391
  12.2 4.2 %forward_cosine.3 = (f32[32,16,128]{2,1,0:T(8,128)S(1)}, f32[32,16,128]{2,1,0:T(8,128)S(1)}) custom-call(s32[512]{0:T(512)S(1)} %reshape.7.sel_in, bf16[128,128,128]{2,1,0:T(8,128)(2,1)} %bitcast.5, bf16[128,128,128]{2,1,0:T(8,128)(2,1)} %bitcast.9, bf16[128,128]{1,0:T(8,128)(2,1)S(1)} %copy-done.2, bf16[128,128]{1,0:T(8,128)(2,1)S(1)} %copy-done.1, ...), custom_call_target="tpu_custom_call" | custom-call | flops 2147483648 | bytes 5242880 | tf_op jit(solution)/shard_map/forward_cosine/pallas_call | solution.py:191
  16.5 0.2 combine.1
  16.7 1.3 %collective-permute-start.2 = (f32[32,16,128]{2,1,0:T(8,128)S(1)}, f32[32,16,128]{2,1,0:T(8,128)S(1)}, u32[]{:S(2)}, u32[]{:S(2)}) collective-permute-start(f32[32,16,128]{2,1,0:T(8,128)S(1)} %get-tuple-element.33.refs_3_), channel_id=1, source_target_pairs={{0,4},{4,0},{8,12},{12,8},{16,20},{20,16},{24,28},{28,24},{32,36},... | collective-permute-start | bytes 786440 | tf_op jit(solution)/shard_map/ppermute | solution.py:384
  18.0 1.2 %collective-permute-done.2 = f32[32,16,128]{2,1,0:T(8,128)S(1)} collective-permute-done((f32[32,16,128]{2,1,0:T(8,128)S(1)}, f32[32,16,128]{2,1,0:T(8,128)S(1)}, u32[]{:S(2)}, u32[]{:S(2)}) %collective-permute-start.2) | collective-permute-done | bytes 262176 | tf_op jit(solution)/shard_map/ppermute | solution.py:384
  19.2 0.7 %add.7 = f32[32,16,128]{2,1,0:T(8,128)} add(f32[32,16,128]{2,1,0:T(8,128)S(1)} %get-tuple-element.38.refs_3_, f32[32,16,128]{2,1,0:T(8,128)S(1)} %collective-permute-done.2) | non-fusion elementwise | flops 65536 | bytes 786432 | tf_op jit(solution)/shard_map/add | solution.py:394
  19.9 13.3 %all-to-all-start = ((f32[32,16,128]{2,1,0:T(8,128)}), f32[32,16,128]{2,1,0:T(8,128)S(1)}, u32[]{:S(2)}, u32[]{:S(2)}) async-start(f32[32,16,128]{2,1,0:T(8,128)} %add.7), calls=%async_computation | async-start | bytes 524288 | tf_op jit(solution)/shard_map/all_to_all | solution.py:385
  33.2 0.1 copy.16
  33.4 0.2 broadcast_in_dim.6
  33.6 0.2 reshape_reshape.3.refs_4_.refs_3_
  33.8 3.9 %momentum_other.1.refs_8_ = bf16[128,128,128]{2,1,0:T(8,128)(2,1)} custom-call(s32[512]{0:T(512)S(1)} %reshape.7.sel_in, bf16[128,128,128]{2,1,0:T(8,128)(2,1)} %bitcast.6, bf16[128,128,128]{2,1,0:T(8,128)(2,1)} %bitcast.10, f32[1,128]{1,0:T(1,128)S(1)} %get-tuple-element.29.refs_2_.refs_1_, f32[32,16,128]{2,1,0:T(8,128)S(1)} %get-tuple-element.33.refs_3_, ...), custom_call_target="tpu_custom_call" | custom-call | flops 2147483648 | bytes 6291456 | tf_op jit(solution)/shard_map/momentum_other/pallas_call | solution.py:332
  37.7 2.2 %all-to-all-done.parts = f32[32,16,128]{2,1,0:T(8,128)S(1)} async-done(((f32[32,16,128]{2,1,0:T(8,128)}), f32[32,16,128]{2,1,0:T(8,128)S(1)}, u32[]{:S(2)}, u32[]{:S(2)}) %all-to-all-start) | async-done | bytes 262176 | tf_op jit(solution)/shard_map/all_to_all | solution.py:385
  39.9 0.9 %scaled_totals.1 = f32[32,16,128]{2,1,0:T(8,128)} custom-call(f32[32,16,128]{2,1,0:T(8,128)S(1)} %all-to-all-done.parts), custom_call_target="tpu_custom_call" | custom-call | flops 1048576 | bytes 524288 | tf_op jit(solution)/shard_map/scaled_totals/pallas_call | solution.py:363
  40.8 9.4 %all-to-all-start.1 = ((f32[32,16,128]{2,1,0:T(8,128)}), f32[32,16,128]{2,1,0:T(8,128)S(1)}, u32[]{:S(2)}, u32[]{:S(2)}) async-start(f32[32,16,128]{2,1,0:T(8,128)} %scaled_totals.1), calls=%async_computation.1 | async-start | bytes 524288 | tf_op jit(solution)/shard_map/all_to_all | solution.py:385
  50.1 3.9 %momentum_own.1 = bf16[128,128,128]{2,1,0:T(8,128)(2,1)} custom-call(s32[512]{0:T(512)S(1)} %reshape.7.sel_in, bf16[128,128,128]{2,1,0:T(8,128)(2,1)} %bitcast.7, bf16[128,128,128]{2,1,0:T(8,128)(2,1)} %bitcast.11, f32[1,128]{1,0:T(1,128)S(1)} %get-tuple-element.29.refs_2_.refs_1_, ...), custom_call_target="tpu_custom_call", output_to_operand_aliasing={{}: (9, {})} | custom-call | flops 2147483648 | bytes 6291456 | tf_op jit(solution)/shard_map/momentum_own/pallas_call | solution.py:332
  54.1 1.3 %all-to-all-done.1.refs_2_ = f32[32,16,128]{2,1,0:T(8,128)S(1)} async-done(((f32[32,16,128]{2,1,0:T(8,128)}), f32[32,16,128]{2,1,0:T(8,128)S(1)}, u32[]{:S(2)}, u32[]{:S(2)}) %all-to-all-start.1) | async-done | bytes 262176 | tf_op jit(solution)/shard_map/all_to_all | solution.py:385
  55.4 2.3 %collective-permute-start.3 = (f32[32,16,128]{2,1,0:T(8,128)S(1)}, f32[32,16,128]{2,1,0:T(8,128)S(1)}, u32[]{:S(2)}, u32[]{:S(2)}) collective-permute-start(f32[32,16,128]{2,1,0:T(8,128)S(1)} %all-to-all-done.1.refs_2_), channel_id=1, source_target_pairs={{0,4},{4,0},{8,12},{12,8},{16,20},{20,16},{24,28},{28,24},{32,36},... | collective-permute-start | bytes 786440 | tf_op jit(solution)/shard_map/ppermute | solution.py:384
  57.7 3.5 %weight_own.1.refs_7_ = bf16[128,128,128]{2,1,0:T(8,128)(2,1)} custom-call(s32[512]{0:T(512)S(1)} %reshape.7.sel_in, bf16[128,128,128]{2,1,0:T(8,128)(2,1)} %refs_0_.3, f32[1,128]{1,0:T(1,128)S(1)} %get-tuple-element.29.refs_2_.refs_1_, f32[32,16,128]{2,1,0:T(8,128)S(1)} %all-to-all-done.1.refs_2_, s32[64,128]{1,0:T(8,128)S(1)} %reshape_reshape.3.refs_4_.refs_3_, ...), custom_call_target="tpu_custom_call" | custom-call | flops 2147483648 | bytes 4194304 | tf_op jit(solution)/shard_map/weight_own/pallas_call | solution.py:332
  61.3 3.6 %weight_other.1 = bf16[128,128,128]{2,1,0:T(8,128)(2,1)} custom-call(s32[512]{0:T(512)S(1)} %reshape.7.sel_in, bf16[128,128,128]{2,1,0:T(8,128)(2,1)} %refs_0_.3, f32[1,128]{1,0:T(1,128)S(1)} %get-tuple-element.29.refs_2_.refs_1_, f32[32,16,128]{2,1,0:T(8,128)S(1)} %collective-permute-done.3.refs_2_, ...), custom_call_target="tpu_custom_call", output_to_operand_aliasing={{}: (8, {})} | custom-call | flops 2147483648 | bytes 4194304 | tf_op jit(solution)/shard_map/weight_other/pallas_call | solution.py:332
  (15 shorter events, 0.0 us)
Async XLA Ops:
  0.6 4.7 %copy-start.1 = (bf16[128,128]{1,0:T(8,128)(2,1)S(1)}, bf16[128,128]{1,0:T(8,128)(2,1)}, u32[]{:S(2)}) copy-start(bf16[128,128]{1,0:T(8,128)(2,1)} %constant.12.clone.t_low.refs_6_.refs_5_) | copy-start | bytes 98308
  0.6 4.7 %copy-start.2 = (bf16[128,128]{1,0:T(8,128)(2,1)S(1)}, bf16[128,128]{1,0:T(8,128)(2,1)}, u32[]{:S(2)}) copy-start(bf16[128,128]{1,0:T(8,128)(2,1)} %constant.11.clone.t_high.refs_5_.refs_4_) | copy-start | bytes 98308
  0.7 4.7 %copy-start.3 = (bf16[256,256]{1,0:T(8,128)(2,1)S(1)}, bf16[256,256]{1,0:T(8,128)(2,1)}, u32[]{:S(2)}) copy-start(bf16[256,256]{1,0:T(8,128)(2,1)} %constant.10.clone.t_right) | copy-start | bytes 393220
  0.7 4.4 %copy-start.4 = (s32[128,4]{0,1:T(4,128)S(1)}, s32[128,4]{0,1:T(4,128)}, u32[]{:S(2)}) copy-start(s32[128,4]{0,1:T(4,128)} %param.11) | copy-start | bytes 6148
  3.0 6.7 %collective-permute-start = (f32[8,128]{1,0:T(8,128)S(1)}, f32[8,128]{1,0:T(8,128)S(1)}, u32[]{:S(2)}, u32[]{:S(2)}) collective-permute-start(f32[8,128]{1,0:T(8,128)S(1)} %square_sums.1), channel_id=1, source_target_pairs={{0,1},{1,0},{2,3},{3,2},{4,5},{5,4},{6,7},{7,6},{8,9},{9,8},{10,11... | collective-permute-start | bytes 12296 | tf_op jit(solution)/shard_map/ppermute | solution.py:388
  9.7 24.1 %copy-start = (bf16[128,384]{1,0:T(8,128)(2,1)S(1)}, bf16[128,384]{1,0:T(8,128)(2,1)}, u32[]{:S(2)}) copy-start(bf16[128,384]{1,0:T(8,128)(2,1)} %constant.13.clone.refs_7_.refs_6_) | copy-start | bytes 294916
  9.7 6.8 %collective-permute-start.1 = (f32[8,128]{1,0:T(8,128)S(1)}, f32[8,128]{1,0:T(8,128)S(1)}, u32[]{:S(2)}, u32[]{:S(2)}) collective-permute-start(f32[8,128]{1,0:T(8,128)S(1)} %add.6.first), channel_id=1, source_target_pairs={{0,2},{1,3},{2,0},{3,1},{4,6},{5,7},{6,4},{7,5},{8,10},{9,11},{10,... | collective-permute-start | bytes 12296 | tf_op jit(solution)/shard_map/ppermute | solution.py:391
  16.7 2.5 %collective-permute-start.2 = (f32[32,16,128]{2,1,0:T(8,128)S(1)}, f32[32,16,128]{2,1,0:T(8,128)S(1)}, u32[]{:S(2)}, u32[]{:S(2)}) collective-permute-start(f32[32,16,128]{2,1,0:T(8,128)S(1)} %get-tuple-element.33.refs_3_), channel_id=1, source_target_pairs={{0,4},{4,0},{8,12},{12,8},{16,20},{20,16},{24,28},{28,24},{32,36},... | collective-permute-start | bytes 786440 | tf_op jit(solution)/shard_map/ppermute | solution.py:384
  19.9 20.0 %all-to-all-start = ((f32[32,16,128]{2,1,0:T(8,128)}), f32[32,16,128]{2,1,0:T(8,128)S(1)}, u32[]{:S(2)}, u32[]{:S(2)}) async-start(f32[32,16,128]{2,1,0:T(8,128)} %add.7), calls=%async_computation | async-start | bytes 524288 | tf_op jit(solution)/shard_map/all_to_all | solution.py:385
  40.8 14.7 %all-to-all-start.1 = ((f32[32,16,128]{2,1,0:T(8,128)}), f32[32,16,128]{2,1,0:T(8,128)S(1)}, u32[]{:S(2)}, u32[]{:S(2)}) async-start(f32[32,16,128]{2,1,0:T(8,128)} %scaled_totals.1), calls=%async_computation.1 | async-start | bytes 524288 | tf_op jit(solution)/shard_map/all_to_all | solution.py:385
  55.4 5.8 %collective-permute-start.3 = (f32[32,16,128]{2,1,0:T(8,128)S(1)}, f32[32,16,128]{2,1,0:T(8,128)S(1)}, u32[]{:S(2)}, u32[]{:S(2)}) collective-permute-start(f32[32,16,128]{2,1,0:T(8,128)S(1)} %all-to-all-done.1.refs_2_), channel_id=1, source_target_pairs={{0,4},{4,0},{8,12},{12,8},{16,20},{20,16},{24,28},{28,24},{32,36},... | collective-permute-start | bytes 786440 | tf_op jit(solution)/shard_map/ppermute | solution.py:384

commit v6 on v5

--- a/solution.py
+++ b/solution.py
@@ -52,12 +52,18 @@
     )
 
 
+def block_at(sel, pair, q):
+    if len(sel.shape) == 1:
+        return sel[pair * 8 + q]
+    return sel[q % KSEL, 2 * pair + q // KSEL]
+
+
 def rows_of(sel, pair):
-    return [lax.shift_right_logical(sel[pair * 8 + q], 3) for q in range(8)]
+    return [lax.shift_right_logical(block_at(sel, pair, q), 3) for q in range(8)]
 
 
 def cols_of(sel, pair):
-    return [lax.bitwise_and(sel[pair * 8 + q], NBS - 1) for q in range(8)]
+    return [lax.bitwise_and(block_at(sel, pair, q), NBS - 1) for q in range(8)]
 
 
 ANY = pl.BlockSpec(memory_space=pl.ANY)
@@ -196,7 +202,7 @@
         scratch_shapes=[
             buf,
             buf,
-            pltpu.SMEM((2 * PAIRS * KSEL,), jnp.int32),
+            pltpu.SMEM((KSEL, 2 * PAIRS), jnp.int32),
             pltpu.SemaphoreType.DMA((2, CHUNKS)),
             pltpu.SemaphoreType.DMA,
         ],
@@ -353,8 +359,10 @@
     total = jnp.sum(parts[...], axis=0)
     lane = lax.broadcasted_iota(jnp.int32, (FB, GROUP), 1)
     square = total * total
-    first = jnp.sum(jnp.where(lane < 64, square, 0.0))
-    second = jnp.sum(jnp.where(lane < 64, 0.0, square))
+    square = jnp.sum(square, axis=0, keepdims=True)
+    lane = lane[:1]
+    first = jnp.sum(jnp.where(lane < 64, square, 0.0), axis=1, keepdims=True)
+    second = jnp.sum(jnp.where(lane < 64, 0.0, square), axis=1, keepdims=True)
     mean = jnp.where(lane < 64, first, second) / (GROUP * GROUP)
     out[...] = jnp.broadcast_to(learn_rate * total * lax.rsqrt(mean + eps), out.shape)
 
@@ -378,7 +386,6 @@
     t_right = jnp.asarray(np.concatenate([right[:, : 2 * GROUP], right[:, 2 * GROUP :]], axis=0))
     t_high, t_low, t_left = tables = tuple(jnp.asarray(table) for table in (high, low, left))
     grads, momentum = grads[0], momentum[0]
-    sel = select.reshape(-1)
     same_core = [[(c + 2 * (18 + k)) % REPS for k in range(CHIPS)] for c in range(2)]
     swap_core = [(i, i ^ 1) for i in range(REPS)]
     swap = lambda x: lax.ppermute(x, "rep", swap_core)
@@ -386,13 +393,14 @@
 
     sums = square_sums(grads)
     sums += lax.ppermute(sums, "mdl", [(i, i ^ 1) for i in range(4)])
-    g_other, m_other = forward(sel, True, grads, momentum, t_high, t_low, t_right)
+    g_other, m_other = forward(select.T, True, grads, momentum, t_high, t_low, t_right)
     sums, g_other, m_other = lax.optimization_barrier((sums, g_other, m_other))
     far = lax.ppermute(sums, "mdl", [(i, i ^ 2) for i in range(4)])
-    g_own, m_own = forward(sel, False, grads, momentum, t_high, t_low, t_right)
+    g_own, m_own = forward(select.T, False, grads, momentum, t_high, t_low, t_right)
     c_other, c_own, clip = combine(sums, far, g_other, m_other, g_own, m_own)
     chip, c_other, c_own = lax.optimization_barrier((c_own + swap(c_other), c_other, c_own))
     select, _ = lax.optimization_barrier((select, chip))
+    sel = select.reshape(-1)
     row_of = jnp.repeat(lax.shift_right_logical(select, 3), FB, axis=1).reshape(PAIRS, GROUP)
     parts = exchange(chip)
     new_momentum = decode_half(

time: 65.1 us -> 64.9 us (level)
  no operation moved by 1% of the time
where the time goes in v6:
time: 64.9 us; the launch traced here: 64.6 us
  starting transfers between devices  31 us (48%)
  Pallas kernels  26.9 us (41%)
  waiting for transfers between devices  4.44 us (7%)
  between operations  0.8 us (1%)
  local copies, waits for them, and re-layouts  0.75 us (1%)
  other arithmetic  0.74 us (1%)
    all_to_all x2, starting transfers between devices, per_device(): lax.all_to_all(x, 'rep', 0, 0, tiled=True, axis_index_groups=same_core)  22.7 us
    pallas_call x4, Pallas kernels, decode_half(): pl.pallas_call(functools.partial(decode_kernel, len(arrays), swapped), in...  15 us
    pallas_call x2, Pallas kernels, forward(): pl.pallas_call(functools.partial(forward_kernel, swapped), in_specs=[ANY]...  8.56 us
    ppermute x2, starting transfers between devices, per_device(): swap = lambda x: lax.ppermute(x, 'rep', swap_core)  3.6 us
    all_to_all x2, waiting for transfers between devices, per_device(): lax.all_to_all(x, 'rep', 0, 0, tiled=True, axis_index_groups=same_core)  3.27 us
    ppermute x1, starting transfers between devices, per_device(): far = lax.ppermute(sums, 'mdl', [(i, i ^ 2) for i in range(4)])  2.54 us
    pallas_call x1, Pallas kernels, square_sums(): pl.pallas_call(square_kernel, in_specs=[ANY], out_specs=VMEM, out_shape=j...  2.29 us
    ppermute x1, starting transfers between devices, per_device(): sums += lax.ppermute(sums, 'mdl', [(i, i ^ 1) for i in range(4)])  2.13 us
  transfers between devices with their start and end apart: 6, of which 3 were waited for; matrix products, arithmetic and copies ran while one was open for 1% of the time, Pallas kernels for 31%

profile of v6, /device:TPU:1, one launch (start us, length us, event | category | flops | bytes accessed | tf_op | source)
XLA Modules:
  0.0 64.6 jit_solution(14210559451554153239)
XLA Ops:
  0.7 2.3 %square_sums.1 = f32[8,128]{1,0:T(8,128)S(1)} custom-call(bf16[128,128,128]{2,1,0:T(8,128)(2,1)} %bitcast.6), custom_call_target="tpu_custom_call" | custom-call | flops 4194304 | bytes 4194304 | tf_op jit(solution)/shard_map/square_sums/pallas_call | solution.py:99
  3.0 2.1 %collective-permute-start = (f32[8,128]{1,0:T(8,128)S(1)}, f32[8,128]{1,0:T(8,128)S(1)}, u32[]{:S(2)}, u32[]{:S(2)}) collective-permute-start(f32[8,128]{1,0:T(8,128)S(1)} %square_sums.1), channel_id=1, source_target_pairs={{0,1},{1,0},{2,3},{3,2},{4,5},{5,4},{6,7},{7,6},{8,9},{9,8},{10,11... | collective-permute-start | bytes 12296 | tf_op jit(solution)/shard_map/ppermute | solution.py:395
  5.1 4.3 %forward_cosine.2 = (f32[32,16,128]{2,1,0:T(8,128)S(1)}, f32[32,16,128]{2,1,0:T(8,128)S(1)}) custom-call(s32[4,128]{1,0:T(4,128)S(1)} %bitcast.4, bf16[128,128,128]{2,1,0:T(8,128)(2,1)} %bitcast.7, bf16[128,128,128]{2,1,0:T(8,128)(2,1)} %bitcast.11, bf16[128,128]{1,0:T(8,128)(2,1)S(1)} %copy-done.2, bf16[128,128]{1,0:T(8,128)(2,1)S(1)} %copy-done.1, ...), custom_call_target="tpu_custom_call" | custom-call | flops 2147483648 | bytes 5242880 | tf_op jit(solution)/shard_map/forward_cosine/pallas_call | solution.py:197
  9.4 2.5 %collective-permute-start.1 = (f32[8,128]{1,0:T(8,128)S(1)}, f32[8,128]{1,0:T(8,128)S(1)}, u32[]{:S(2)}, u32[]{:S(2)}) collective-permute-start(f32[8,128]{1,0:T(8,128)S(1)} %add.6.first), channel_id=1, source_target_pairs={{0,2},{1,3},{2,0},{3,1},{4,6},{5,7},{6,4},{7,5},{8,10},{9,11},{10,... | collective-permute-start | bytes 12296 | tf_op jit(solution)/shard_map/ppermute | solution.py:398
  12.0 4.3 %forward_cosine.3 = (f32[32,16,128]{2,1,0:T(8,128)S(1)}, f32[32,16,128]{2,1,0:T(8,128)S(1)}) custom-call(s32[4,128]{1,0:T(4,128)S(1)} %bitcast.5, bf16[128,128,128]{2,1,0:T(8,128)(2,1)} %bitcast.8, bf16[128,128,128]{2,1,0:T(8,128)(2,1)} %bitcast.12, bf16[128,128]{1,0:T(8,128)(2,1)S(1)} %copy-done.2, bf16[128,128]{1,0:T(8,128)(2,1)S(1)} %copy-done.1, ...), custom_call_target="tpu_custom_call" | custom-call | flops 2147483648 | bytes 5242880 | tf_op jit(solution)/shard_map/forward_cosine/pallas_call | solution.py:197
  16.3 0.2 combine.1
  16.5 1.3 %collective-permute-start.2 = (f32[32,16,128]{2,1,0:T(8,128)S(1)}, f32[32,16,128]{2,1,0:T(8,128)S(1)}, u32[]{:S(2)}, u32[]{:S(2)}) collective-permute-start(f32[32,16,128]{2,1,0:T(8,128)S(1)} %get-tuple-element.34.refs_3_), channel_id=1, source_target_pairs={{0,4},{4,0},{8,12},{12,8},{16,20},{20,16},{24,28},{28,24},{32,36},... | collective-permute-start | bytes 786440 | tf_op jit(solution)/shard_map/ppermute | solution.py:391
  17.8 1.2 %collective-permute-done.2 = f32[32,16,128]{2,1,0:T(8,128)S(1)} collective-permute-done((f32[32,16,128]{2,1,0:T(8,128)S(1)}, f32[32,16,128]{2,1,0:T(8,128)S(1)}, u32[]{:S(2)}, u32[]{:S(2)}) %collective-permute-start.2) | collective-permute-done | bytes 262176 | tf_op jit(solution)/shard_map/ppermute | solution.py:391
  19.0 0.7 %add.7 = f32[32,16,128]{2,1,0:T(8,128)} add(f32[32,16,128]{2,1,0:T(8,128)S(1)} %get-tuple-element.38.refs_3_, f32[32,16,128]{2,1,0:T(8,128)S(1)} %collective-permute-done.2) | non-fusion elementwise | flops 65536 | bytes 786432 | tf_op jit(solution)/shard_map/add | solution.py:401
  19.7 13.3 %all-to-all-start = ((f32[32,16,128]{2,1,0:T(8,128)}), f32[32,16,128]{2,1,0:T(8,128)S(1)}, u32[]{:S(2)}, u32[]{:S(2)}) async-start(f32[32,16,128]{2,1,0:T(8,128)} %add.7), calls=%async_computation | async-start | bytes 524288 | tf_op jit(solution)/shard_map/all_to_all | solution.py:392
  33.1 0.1 copy.15
  33.2 0.1 copy.16
  33.3 0.1 reshape.7.sel_in
  33.4 0.2 broadcast_in_dim.6
  33.6 0.2 reshape_reshape.3.refs_4_.refs_3_
  33.8 3.9 %momentum_other.1.refs_8_ = bf16[128,128,128]{2,1,0:T(8,128)(2,1)} custom-call(s32[512]{0:T(512)S(1)} %reshape.7.sel_in, bf16[128,128,128]{2,1,0:T(8,128)(2,1)} %bitcast.9, bf16[128,128,128]{2,1,0:T(8,128)(2,1)} %bitcast.13, f32[1,128]{1,0:T(1,128)S(1)} %get-tuple-element.33.refs_2_.refs_1_, f32[32,16,128]{2,1,0:T(8,128)S(1)} %get-tuple-element.34.refs_3_, ...), custom_call_target="tpu_custom_call" | custom-call | flops 2147483648 | bytes 6291456 | tf_op jit(solution)/shard_map/momentum_other/pallas_call | solution.py:338
  37.7 2.0 %all-to-all-done.parts = f32[32,16,128]{2,1,0:T(8,128)S(1)} async-done(((f32[32,16,128]{2,1,0:T(8,128)}), f32[32,16,128]{2,1,0:T(8,128)S(1)}, u32[]{:S(2)}, u32[]{:S(2)}) %all-to-all-start) | async-done | bytes 262176 | tf_op jit(solution)/shard_map/all_to_all | solution.py:392
  39.7 0.8 %scaled_totals.1 = f32[32,16,128]{2,1,0:T(8,128)} custom-call(f32[32,16,128]{2,1,0:T(8,128)S(1)} %all-to-all-done.parts), custom_call_target="tpu_custom_call" | custom-call | flops 1048576 | bytes 524288 | tf_op jit(solution)/shard_map/scaled_totals/pallas_call | solution.py:371
  40.5 9.4 %all-to-all-start.1 = ((f32[32,16,128]{2,1,0:T(8,128)}), f32[32,16,128]{2,1,0:T(8,128)S(1)}, u32[]{:S(2)}, u32[]{:S(2)}) async-start(f32[32,16,128]{2,1,0:T(8,128)} %scaled_totals.1), calls=%async_computation.1 | async-start | bytes 524288 | tf_op jit(solution)/shard_map/all_to_all | solution.py:392
  49.9 3.9 %momentum_own.1 = bf16[128,128,128]{2,1,0:T(8,128)(2,1)} custom-call(s32[512]{0:T(512)S(1)} %reshape.7.sel_in, bf16[128,128,128]{2,1,0:T(8,128)(2,1)} %bitcast.10, bf16[128,128,128]{2,1,0:T(8,128)(2,1)} %bitcast.14, f32[1,128]{1,0:T(1,128)S(1)} %get-tuple-element.33.refs_2_.refs_1_, ...), custom_call_target="tpu_custom_call", output_to_operand_aliasing={{}: (9, {})} | custom-call | flops 2147483648 | bytes 6291456 | tf_op jit(solution)/shard_map/momentum_own/pallas_call | solution.py:338
  53.9 1.3 %all-to-all-done.1.refs_2_ = f32[32,16,128]{2,1,0:T(8,128)S(1)} async-done(((f32[32,16,128]{2,1,0:T(8,128)}), f32[32,16,128]{2,1,0:T(8,128)S(1)}, u32[]{:S(2)}, u32[]{:S(2)}) %all-to-all-start.1) | async-done | bytes 262176 | tf_op jit(solution)/shard_map/all_to_all | solution.py:392
  55.2 2.3 %collective-permute-start.3 = (f32[32,16,128]{2,1,0:T(8,128)S(1)}, f32[32,16,128]{2,1,0:T(8,128)S(1)}, u32[]{:S(2)}, u32[]{:S(2)}) collective-permute-start(f32[32,16,128]{2,1,0:T(8,128)S(1)} %all-to-all-done.1.refs_2_), channel_id=1, source_target_pairs={{0,4},{4,0},{8,12},{12,8},{16,20},{20,16},{24,28},{28,24},{32,36},... | collective-permute-start | bytes 786440 | tf_op jit(solution)/shard_map/ppermute | solution.py:391
  57.5 3.5 %weight_own.1.refs_7_ = bf16[128,128,128]{2,1,0:T(8,128)(2,1)} custom-call(s32[512]{0:T(512)S(1)} %reshape.7.sel_in, bf16[128,128,128]{2,1,0:T(8,128)(2,1)} %refs_0_.3, f32[1,128]{1,0:T(1,128)S(1)} %get-tuple-element.33.refs_2_.refs_1_, f32[32,16,128]{2,1,0:T(8,128)S(1)} %all-to-all-done.1.refs_2_, s32[64,128]{1,0:T(8,128)S(1)} %reshape_reshape.3.refs_4_.refs_3_, ...), custom_call_target="tpu_custom_call" | custom-call | flops 2147483648 | bytes 4194304 | tf_op jit(solution)/shard_map/weight_own/pallas_call | solution.py:338
  61.0 3.6 %weight_other.1 = bf16[128,128,128]{2,1,0:T(8,128)(2,1)} custom-call(s32[512]{0:T(512)S(1)} %reshape.7.sel_in, bf16[128,128,128]{2,1,0:T(8,128)(2,1)} %refs_0_.3, f32[1,128]{1,0:T(1,128)S(1)} %get-tuple-element.33.refs_2_.refs_1_, f32[32,16,128]{2,1,0:T(8,128)S(1)} %collective-permute-done.3.refs_2_, ...), custom_call_target="tpu_custom_call", output_to_operand_aliasing={{}: (8, {})} | custom-call | flops 2147483648 | bytes 4194304 | tf_op jit(solution)/shard_map/weight_other/pallas_call | solution.py:338
  (15 shorter events, 0.0 us)
Async XLA Ops:
  0.6 4.5 %copy-start.1 = (bf16[128,128]{1,0:T(8,128)(2,1)S(1)}, bf16[128,128]{1,0:T(8,128)(2,1)}, u32[]{:S(2)}) copy-start(bf16[128,128]{1,0:T(8,128)(2,1)} %constant.12.clone.t_low.refs_6_.refs_5_) | copy-start | bytes 98308
  0.6 4.5 %copy-start.2 = (bf16[128,128]{1,0:T(8,128)(2,1)S(1)}, bf16[128,128]{1,0:T(8,128)(2,1)}, u32[]{:S(2)}) copy-start(bf16[128,128]{1,0:T(8,128)(2,1)} %constant.11.clone.t_high.refs_5_.refs_4_) | copy-start | bytes 98308
  0.7 4.5 %copy-start.3 = (bf16[256,256]{1,0:T(8,128)(2,1)S(1)}, bf16[256,256]{1,0:T(8,128)(2,1)}, u32[]{:S(2)}) copy-start(bf16[256,256]{1,0:T(8,128)(2,1)} %constant.10.clone.t_right) | copy-start | bytes 393220
  0.7 4.4 %copy-start.4 = (s32[128,4]{0,1:T(4,128)S(1)}, s32[128,4]{0,1:T(4,128)}, u32[]{:S(2)}) copy-start(s32[128,4]{0,1:T(4,128)} %param.11) | copy-start | bytes 6148
  3.0 6.4 %collective-permute-start = (f32[8,128]{1,0:T(8,128)S(1)}, f32[8,128]{1,0:T(8,128)S(1)}, u32[]{:S(2)}, u32[]{:S(2)}) collective-permute-start(f32[8,128]{1,0:T(8,128)S(1)} %square_sums.1), channel_id=1, source_target_pairs={{0,1},{1,0},{2,3},{3,2},{4,5},{5,4},{6,7},{7,6},{8,9},{9,8},{10,11... | collective-permute-start | bytes 12296 | tf_op jit(solution)/shard_map/ppermute | solution.py:395
  9.4 24.4 %copy-start = (bf16[128,384]{1,0:T(8,128)(2,1)S(1)}, bf16[128,384]{1,0:T(8,128)(2,1)}, u32[]{:S(2)}) copy-start(bf16[128,384]{1,0:T(8,128)(2,1)} %constant.13.clone.refs_7_.refs_6_) | copy-start | bytes 294916
  9.4 6.8 %collective-permute-start.1 = (f32[8,128]{1,0:T(8,128)S(1)}, f32[8,128]{1,0:T(8,128)S(1)}, u32[]{:S(2)}, u32[]{:S(2)}) collective-permute-start(f32[8,128]{1,0:T(8,128)S(1)} %add.6.first), channel_id=1, source_target_pairs={{0,2},{1,3},{2,0},{3,1},{4,6},{5,7},{6,4},{7,5},{8,10},{9,11},{10,... | collective-permute-start | bytes 12296 | tf_op jit(solution)/shard_map/ppermute | solution.py:398
  16.5 2.5 %collective-permute-start.2 = (f32[32,16,128]{2,1,0:T(8,128)S(1)}, f32[32,16,128]{2,1,0:T(8,128)S(1)}, u32[]{:S(2)}, u32[]{:S(2)}) collective-permute-start(f32[32,16,128]{2,1,0:T(8,128)S(1)} %get-tuple-element.34.refs_3_), channel_id=1, source_target_pairs={{0,4},{4,0},{8,12},{12,8},{16,20},{20,16},{24,28},{28,24},{32,36},... | collective-permute-start | bytes 786440 | tf_op jit(solution)/shard_map/ppermute | solution.py:391
  19.7 20.0 %all-to-all-start = ((f32[32,16,128]{2,1,0:T(8,128)}), f32[32,16,128]{2,1,0:T(8,128)S(1)}, u32[]{:S(2)}, u32[]{:S(2)}) async-start(f32[32,16,128]{2,1,0:T(8,128)} %add.7), calls=%async_computation | async-start | bytes 524288 | tf_op jit(solution)/shard_map/all_to_all | solution.py:392
  40.5 14.7 %all-to-all-start.1 = ((f32[32,16,128]{2,1,0:T(8,128)}), f32[32,16,128]{2,1,0:T(8,128)S(1)}, u32[]{:S(2)}, u32[]{:S(2)}) async-start(f32[32,16,128]{2,1,0:T(8,128)} %scaled_totals.1), calls=%async_computation.1 | async-start | bytes 524288 | tf_op jit(solution)/shard_map/all_to_all | solution.py:392
  55.2 5.8 %collective-permute-start.3 = (f32[32,16,128]{2,1,0:T(8,128)S(1)}, f32[32,16,128]{2,1,0:T(8,128)S(1)}, u32[]{:S(2)}, u32[]{:S(2)}) collective-permute-start(f32[32,16,128]{2,1,0:T(8,128)S(1)} %all-to-all-done.1.refs_2_), channel_id=1, source_target_pairs={{0,4},{4,0},{8,12},{12,8},{16,20},{20,16},{24,28},{28,24},{32,36},... | collective-permute-start | bytes 786440 | tf_op jit(solution)/shard_map/ppermute | solution.py:391
